TPU v7x, 256 devices: a whole 4x4x8 slice. The times are simulated.
256 devices in a mesh: src: 16 (over y, z_hi, core), tgt: 16 (over z_lo, x).
Axes of the slice: x: 4, y: 4, z: 8 (z_hi: 2, z_lo: 4; z = z_hi * 4 + z_lo), core: 2. Of those that a mesh axis runs over, the one named last changes fastest.
Arguments:
- sources: bfloat16 [32768, 128], P(('src', 'tgt')), may hold values from -4 to 4
- targets: bfloat16 [32768, 128], P('tgt'), may hold values from -4 to 4
- src_logmass: float32 [32768], P('src'), may hold values from -4 to 4
- tgt_logmass: float32 [32768], P('tgt'), may hold values from -4 to 4
Outputs:
- mapped: float32 [32768, 128], P(('src', 'tgt'))
- src_dual: float32 [32768], P('src')
- tgt_dual: float32 [32768], P('tgt')
All inputs are finite; a program needn't handle non-finite values.
Results may differ from a plain program's by a relative error of at most 0.0003.
Values may be sent and summed in bfloat16 or wider, within the bound.
A program may use at most 64 MiB of HBM per device.

v0:
```python
import jax
import jax.numpy as jnp
from jax import lax
from jax.sharding import PartitionSpec as P

ITERS = 2


entropy_weight = 0.03125


def shards(sources, targets, src_logmass, tgt_logmass):
    src_codes = lax.all_gather(sources, "tgt", axis=0, tiled=True)
    src_rows = src_codes.shape[0]
    tgt_rows = targets.shape[0]
    features = targets.shape[1]
    block_rows = 512
    block_count = src_rows // block_rows
    src_norm = 0.5 * jnp.sum(jnp.square(src_codes.astype(jnp.float32)), axis=1) / features
    tgt_norm = 0.5 * jnp.sum(jnp.square(targets.astype(jnp.float32)), axis=1) / features
    tgt_float = targets.astype(jnp.float32)
    src_blocks = src_codes.reshape(block_count, block_rows, features)
    norm_blocks = src_norm.reshape(block_count, block_rows)

    def cost_tile(src_block, src_part):
        inner = lax.dot_general(
            src_block, targets, (((1,), (1,)), ((), ())), preferred_element_type=jnp.float32
        )
        return src_part[:, None] + tgt_norm[None, :] - inner / features

    tgt_dual = jnp.zeros((tgt_rows,), jnp.float32)
    src_dual = jnp.zeros((src_rows,), jnp.float32)
    for iteration in range(ITERS):

        def row_stats(inputs, tgt_dual=tgt_dual):
            src_block, src_part = inputs
            scores = (tgt_dual[None, :] - cost_tile(src_block, src_part)) / entropy_weight
            highest = jnp.max(scores, axis=1)
            return (highest, jnp.sum(jnp.exp(scores - highest[:, None]), axis=1))

        row_high, row_sum = lax.map(row_stats, (src_blocks, norm_blocks))
        row_high = row_high.reshape(src_rows)
        row_sum = row_sum.reshape(src_rows)
        whole_high = lax.pmax(row_high, "tgt")
        row_sum = lax.psum(row_sum * jnp.exp(row_high - whole_high), "tgt")
        row_high = whole_high
        src_dual = entropy_weight * (src_logmass - (row_high + jnp.log(row_sum)))
        dual_blocks = src_dual.reshape(block_count, block_rows)

        def col_step(carried, inputs):
            highest, summed = carried
            src_block, src_part, dual_part = inputs
            scores = (dual_part[:, None] - cost_tile(src_block, src_part)) / entropy_weight
            new_high = jnp.maximum(highest, jnp.max(scores, axis=0))
            summed = summed * jnp.exp(highest - new_high) + jnp.sum(
                jnp.exp(scores - new_high[None, :]), axis=0
            )
            return ((new_high, summed), None)

        starting = (
            jnp.full((tgt_rows,), -jnp.inf, jnp.float32),
            jnp.zeros((tgt_rows,), jnp.float32),
        )
        (col_high, col_sum), unused = lax.scan(
            col_step, starting, (src_blocks, norm_blocks, dual_blocks)
        )
        whole_col = lax.pmax(col_high, "src")
        col_sum = lax.psum(col_sum * jnp.exp(col_high - whole_col), "src")
        col_high = whole_col
        tgt_dual = entropy_weight * (tgt_logmass - (col_high + jnp.log(col_sum)))

    def map_terms(inputs):
        src_block, src_part, high_part = inputs
        scores = (tgt_dual[None, :] - cost_tile(src_block, src_part)) / entropy_weight
        weights = jnp.exp(scores - high_part[:, None])
        row_mass = jnp.sum(weights, axis=1)
        row_moment = jnp.dot(
            weights, tgt_float, precision=lax.Precision.HIGHEST, preferred_element_type=jnp.float32
        )
        return (row_moment, row_mass)

    def map_high(inputs):
        src_block, src_part = inputs
        scores = (tgt_dual[None, :] - cost_tile(src_block, src_part)) / entropy_weight
        return jnp.max(scores, axis=1)

    local_high = lax.map(map_high, (src_blocks, norm_blocks)).reshape(src_rows)
    final_high = lax.pmax(local_high, "tgt")
    high_blocks = final_high.reshape(block_count, block_rows)
    row_moment, row_mass = lax.map(map_terms, (src_blocks, norm_blocks, high_blocks))
    row_moment = row_moment.reshape(src_rows, features)
    row_mass = row_mass.reshape(src_rows)
    all_moment, all_mass = lax.psum((row_moment, row_mass), "tgt")
    share_rows = src_rows // lax.axis_size("tgt")
    offset = lax.axis_index("tgt") * share_rows
    own_moment = lax.dynamic_slice_in_dim(all_moment, offset, share_rows, 0)
    own_mass = lax.dynamic_slice_in_dim(all_mass, offset, share_rows, 0)
    mapped = own_moment / own_mass[:, None]
    return (mapped, src_dual, tgt_dual)


def solution(mesh):
    placed = (P(("src", "tgt"), None), P("tgt", None), P("src"), P("tgt"))
    return jax.shard_map(
        shards,
        mesh=mesh,
        in_specs=placed,
        out_specs=(P(("src", "tgt"), None), P("src"), P("tgt")),
        check_vma=False,
    )
```

profile of v0, /device:TPU:1, one launch (start us, length us, event | category | flops | bytes accessed | tf_op | source)
XLA Modules:
  0.0 695.3 jit_solution(16793808623323705029)
XLA Ops:
  9.8 40.6 %all_gather.3 = bf16[2048,128]{1,0:T(8,128)(2,1)S(1)} all-gather(bf16[128,128]{1,0:T(8,128)(2,1)} %param.16), channel_id=1, replica_groups=mesh['src'=16,'tgt'=16] {'tgt'}, dimensions={0}, use_global_device_ids=true | all-gather | bytes 557056 | tf_op jit(solution)/shard_map/all_gather | solution.py:13
  50.8 12.0 %while.72 = (s32[]{:T(128)}, f32[4,512]{1,0:T(4,128)S(1)}, f32[4,512]{1,0:T(4,128)S(1)}, f32[4,512]{1,0:T(4,128)S(1)}, f32[2048]{0:T(1024)S(1)}, /*index=5*/bf16...) while((s32[]{:T(128)}, f32[4,512]{1,0:T(4,128)S(1)}, f32[4,512]{1,0:T(4,128)S(1)}, ...), condition=%wide.region_5.6_spmd, body=%wide.region_2.5_spmd.sunk | while | flops 276823040 | bytes 9072749 | solution.py:41
  59.7 2.2 fusion.52
  62.7 31.4 %pmax.35 = f32[2048]{0:T(1024)S(1)} all-reduce(f32[2048]{0:T(1024)S(1)} %bitcast.133), channel_id=1, replica_groups=mesh['src'=16,'tgt'=16] {'tgt'}, use_global_device_ids=true, to_apply=%region_6.7 | all-reduce | flops 2048 | bytes 16384 | tf_op jit(solution)/shard_map/pmax | solution.py:44
  94.1 33.1 %psum.42 = f32[2048]{0:T(1024)S(1)} all-reduce(f32[2048]{0:T(1024)S(1)} %exponential_multiply_fusion.3), channel_id=1, replica_groups=mesh['src'=16,'tgt'=16] {'tgt'}, use_global_device_ids=true, to_apply=%region_7.8 | all-reduce | flops 2048 | bytes 16384 | tf_op jit(solution)/shard_map/psum | solution.py:45
  127.3 27.4 %while.76 = (s32[]{:T(128)}, f32[2048]{0:T(1024)S(1)}, f32[2048]{0:T(1024)S(1)}, f32[4,512]{1,0:T(4,128)S(1)}, f32[4,512]{1,0:T(4,128)S(1)}, /*index=5*/f32[2048...) while((s32[]{:T(128)}, f32[2048]{0:T(1024)S(1)}, ...), condition=%wide.region_11.12_spmd.clone, body=%wide.region_8.11_spmd.clone.sunk | while | flops 276834304 | bytes 9171064 | solution.py:64
  127.3 4.0 fusion.63
  131.3 2.8 exponential_reduce_fusion.10
  134.2 4.0 fusion.63
  138.2 2.8 exponential_reduce_fusion.10
  141.0 4.0 fusion.63
  145.0 2.8 exponential_reduce_fusion.10
  147.8 4.0 fusion.63
  151.8 2.8 exponential_reduce_fusion.10
  154.7 64.4 %pmax.36 = f32[2048]{0:T(1024)S(1)} all-reduce(f32[2048]{0:T(1024)S(1)} %get-tuple-element.262), channel_id=1, replica_groups=mesh['src'=16,'tgt'=16] {'src'}, use_global_device_ids=true, to_apply=%region_12.13 | all-reduce | flops 2048 | bytes 16384 | tf_op jit(solution)/shard_map/pmax | solution.py:67
  219.1 43.4 %psum.43 = f32[2048]{0:T(1024)S(1)} all-reduce(f32[2048]{0:T(1024)S(1)} %exponential_multiply_fusion.2), channel_id=1, replica_groups=mesh['src'=16,'tgt'=16] {'src'}, use_global_device_ids=true, to_apply=%region_13.14 | all-reduce | flops 2048 | bytes 16384 | tf_op jit(solution)/shard_map/psum | solution.py:68
  262.6 12.0 %while.73 = (s32[]{:T(128)}, f32[4,512]{1,0:T(4,128)S(1)}, f32[4,512]{1,0:T(4,128)S(1)}, f32[2048]{0:T(1024)S(1)}, f32[4,512]{1,0:T(4,128)S(1)}, /*index=5*/f32[...) while((s32[]{:T(128)}, f32[4,512]{1,0:T(4,128)S(1)}, ...), condition=%wide.region_17.18_spmd, body=%wide.region_14.17_spmd.sunk | while | flops 276823040 | bytes 9080949 | solution.py:41
  262.7 2.2 fusion.54
  265.7 2.2 fusion.54
  268.7 2.2 fusion.54
  271.7 2.2 fusion.54
  274.6 31.4 %pmax.37 = f32[2048]{0:T(1024)S(1)} all-reduce(f32[2048]{0:T(1024)S(1)} %bitcast.135), channel_id=1, replica_groups=mesh['src'=16,'tgt'=16] {'tgt'}, use_global_device_ids=true, to_apply=%region_18.19 | all-reduce | flops 2048 | bytes 16384 | tf_op jit(solution)/shard_map/pmax | solution.py:44
  306.0 33.1 %psum.44 = f32[2048]{0:T(1024)S(1)} all-reduce(f32[2048]{0:T(1024)S(1)} %exponential_multiply_fusion.1), channel_id=1, replica_groups=mesh['src'=16,'tgt'=16] {'tgt'}, use_global_device_ids=true, to_apply=%region_19.20 | all-reduce | flops 2048 | bytes 16384 | tf_op jit(solution)/shard_map/psum | solution.py:45
  339.8 27.3 %while.77 = (s32[]{:T(128)}, f32[2048]{0:T(1024)S(1)}, f32[2048]{0:T(1024)S(1)}, f32[4,512]{1,0:T(4,128)S(1)}, f32[4,512]{1,0:T(4,128)S(1)}, /*index=5*/f32[2048...) while((s32[]{:T(128)}, f32[2048]{0:T(1024)S(1)}, ...), condition=%wide.region_23.24_spmd.clone, body=%wide.region_20.23_spmd.clone.sunk | while | flops 276834304 | bytes 9171064 | solution.py:64
  339.8 4.0 fusion.66
  343.8 2.8 exponential_reduce_fusion.11
  346.6 4.0 fusion.66
  350.6 2.8 exponential_reduce_fusion.11
  353.5 4.0 fusion.66
  357.5 2.8 exponential_reduce_fusion.11
  360.3 4.0 fusion.66
  364.3 2.8 exponential_reduce_fusion.11
  367.1 57.6 %pmax.38 = f32[2048]{0:T(1024)S(1)} all-reduce(f32[2048]{0:T(1024)S(1)} %get-tuple-element.266), channel_id=1, replica_groups=mesh['src'=16,'tgt'=16] {'src'}, use_global_device_ids=true, to_apply=%region_24.25 | all-reduce | flops 2048 | bytes 16384 | tf_op jit(solution)/shard_map/pmax | solution.py:67
  424.7 43.4 %psum.45 = f32[2048]{0:T(1024)S(1)} all-reduce(f32[2048]{0:T(1024)S(1)} %exponential_multiply_fusion), channel_id=1, replica_groups=mesh['src'=16,'tgt'=16] {'src'}, use_global_device_ids=true, to_apply=%region_25.26 | all-reduce | flops 2048 | bytes 16384 | tf_op jit(solution)/shard_map/psum | solution.py:68
  468.1 8.9 %while.74 = (s32[]{:T(128)}, f32[4,512]{1,0:T(4,128)S(1)}, f32[2048]{0:T(1024)S(1)}, f32[4,512]{1,0:T(4,128)S(1)}, f32[2048]{0:T(1024)S(1)}, /*index=5*/bf16[4,5...) while((s32[]{:T(128)}, f32[4,512]{1,0:T(4,128)S(1)}, f32[2048]{0:T(1024)S(1)}, ...), condition=%wide.region_28.29_spmd, body=%wide.region_26.28_spmd.sunk | while | flops 274726400 | bytes 684137 | solution.py:87
  474.8 2.1 multiply_reduce_fusion.4
  477.0 31.5 %pmax.39 = f32[4,512]{1,0:T(4,128)S(1)} all-reduce(f32[4,512]{1,0:T(4,128)S(1)} %get-tuple-element.268), channel_id=1, replica_groups=mesh['src'=16,'tgt'=16] {'tgt'}, use_global_device_ids=true, to_apply=%region_29.30 | all-reduce | flops 2048 | bytes 16384 | tf_op jit(solution)/shard_map/pmax | solution.py:88
  508.5 24.5 %while.75 = (s32[]{:T(128)}, f32[4,512,128]{2,1,0:T(8,128)S(1)}, f32[4,512]{1,0:T(4,128)S(1)}, f32[2048]{0:T(1024)S(1)}, f32[4,512]{1,0:T(4,128)S(1)}, /*index=5...) while((s32[]{:T(128)}, f32[4,512,128]{2,1,0:T(8,128)S(1)}, ...), condition=%wide.region_32.33_spmd, body=%wide.region_30.32_spmd.sunk | while | flops 1886387712 | bytes 10389637 | solution.py:90
  508.6 2.6 fusion.60
  511.2 3.4 fusion.61
  514.7 2.6 fusion.60
  517.3 3.4 fusion.61
  520.8 2.6 fusion.60
  523.4 3.4 fusion.61
  527.0 2.6 fusion.60
  529.6 3.4 fusion.61
  534.1 33.5 %psum.47 = f32[2048]{0:T(1024)S(1)} all-reduce(f32[2048]{0:T(1024)S(1)} %bitcast.148), channel_id=1, replica_groups=mesh['src'=16,'tgt'=16] {'tgt'}, use_global_device_ids=true, to_apply=%region_34.35 | all-reduce | flops 2048 | bytes 16384 | tf_op jit(solution)/shard_map/psum | solution.py:93
  567.7 119.2 %all-reduce.2.cloned.1.call-done = f32[2048,128]{1,0:T(8,128)} async-done(((f32[2048,128]{1,0:T(8,128)}), f32[2048,128]{1,0:T(8,128)}) %all-reduce.2.cloned.1.call-update) | async-done | bytes 1048592 | tf_op jit(solution)/shard_map/psum | solution.py:93
  (132 shorter events, 26.3 us)
Async XLA Ops:
  7.2 679.7 %all-reduce.2.cloned.1.call-start = ((), (), s32[]{:S(2)}) async-start(), calls=%async_computation | async-start | bytes 2097152 | tf_op jit(solution)/shard_map/psum | solution.py:93
  50.7 76.5 %copy-start.2 = (f32[2048]{0:T(1024)S(1)}, f32[2048]{0:T(1024)}, u32[]{:S(2)}) copy-start(f32[2048]{0:T(1024)} %param.18) | copy-start | bytes 24580
  127.3 135.3 %copy-start.3 = (f32[2048]{0:T(1024)S(1)}, f32[2048]{0:T(1024)}, u32[]{:S(2)}) copy-start(f32[2048]{0:T(1024)} %param.19) | copy-start | bytes 24580
  339.2 0.6 copy-start.1
  533.1 1.0 copy-start
  533.1 155.3 %copy-start.4 = (f32[2048]{0:T(1024)}, f32[2048]{0:T(1024)S(1)}, u32[]{:S(2)}) copy-start(f32[2048]{0:T(1024)S(1)} %get-tuple-element.967) | copy-start | bytes 24580
Sparse Core Ops, SparseCore 0:
  534.2 152.5 all-reduce.1
where the time goes:
time: 707 us; the launch traced here: 695 us
  blocking collectives  443 us (63%)
  waiting for transfers between devices  119 us (17%)
  matrix products  81.8 us (12%)
  other arithmetic  32.6 us (5%)
  between operations  14.4 us (2%)
    pmax x2, blocking collectives, shards(): whole_col = lax.pmax(col_high, 'src')  122 us
    psum x1, waiting for transfers between devices, shards(): all_moment, all_mass = lax.psum((row_moment, row_mass), 'tgt')  119 us
    psum x2, blocking collectives, shards(): col_sum = lax.psum(col_sum * jnp.exp(col_high - whole_col), 'src')  86.8 us
    dot_general x24, matrix products, cost_tile(): lax.dot_general(src_block, targets, (((1,), (1,)), ((), ())), preferred_e...  68.1 us
    psum x2, blocking collectives, shards(): row_sum = lax.psum(row_sum * jnp.exp(row_high - whole_high), 'tgt')  66.2 us
    pmax x2, blocking collectives, shards(): whole_high = lax.pmax(row_high, 'tgt')  62.7 us
    all_gather x1, blocking collectives, shards(): src_codes = lax.all_gather(sources, 'tgt', axis=0, tiled=True)  40.6 us
    psum x1, blocking collectives, shards(): all_moment, all_mass = lax.psum((row_moment, row_mass), 'tgt')  33.5 us
  transfers between devices with their start and end apart: 1, of which 1 were waited for; matrix products, arithmetic and copies ran while one was open for 0% of the time, Pallas kernels for 0%

commit v1 on v0

v1 whole, which is shorter than its diff:
```python
import functools
import math

import jax
import jax.numpy as jnp
from jax import lax
from jax.experimental import pallas as pl
from jax.experimental.pallas import tpu as pltpu
from jax.sharding import PartitionSpec as P

MESH = pl.DeviceIdType.MESH
EPS = 0.03125
LOG2E = math.log2(math.e)
B = 128
NB = 16
N = B * NB
D = 128
Q = 4
SCALE = LOG2E / (D * EPS)
BF = jnp.bfloat16
F32 = jnp.float32


def lse_sub(y):
    high = jnp.max(y, axis=0, keepdims=True)
    return high + jnp.log2(jnp.sum(jnp.exp2(y - high), axis=0, keepdims=True))


def tile_high(u):
    m = u[:, :B]
    for k in range(1, NB):
        m = jnp.maximum(m, u[:, k * B : (k + 1) * B])
    return m


def lse_block(lhs, rhs):
    u = jnp.dot(lhs, rhs, preferred_element_type=F32)
    m = tile_high(u)
    s = jnp.exp2((u[:, :B] - m) * SCALE)
    for k in range(1, NB):
        s = s + jnp.exp2((u[:, k * B : (k + 1) * B] - m) * SCALE)
    return lse_sub((m * SCALE + jnp.log2(s)).T)


def kernel(
    src_ref, tgt_ref, slm_ref, tlm_ref, map_ref, sd_ref, td_ref,
    codes, src_t, tgt_t, tgt_one, src_norm, tgt_norm, vec, lo_buf, hi_buf,
    part, got, part2, got2,
    g_hi_send, g_hi_recv, g_lo_send, g_lo_recv,
    e_send, e_recv, m_send, m_recv, r_send, r_recv,
):
    src_me = lax.axis_index("src")
    tgt_me = lax.axis_index("tgt")
    s_hi, s_lo = src_me // Q, src_me % Q
    t_hi, t_lo = tgt_me // Q, tgt_me % Q

    def lo_peer(axis, k):
        hi, lo = (s_hi, s_lo) if axis == "src" else (t_hi, t_lo)
        return {axis: hi * Q + (lo + k) % Q}

    def hi_peer(axis, k):
        hi, lo = (s_hi, s_lo) if axis == "src" else (t_hi, t_lo)
        return {axis: ((hi + k) % Q) * Q + lo}

    barrier = pltpu.get_barrier_semaphore()
    for axis in ("tgt", "src"):
        for k in range(1, Q):
            pl.semaphore_signal(barrier, 1, device_id=lo_peer(axis, k), device_id_type=MESH)
            pl.semaphore_signal(barrier, 1, device_id=hi_peer(axis, k), device_id_type=MESH)

    def copy(src, dst, send, recv, peer):
        return pltpu.make_async_remote_copy(
            src_ref=src, dst_ref=dst, send_sem=send, recv_sem=recv, device_id=peer, device_id_type=MESH
        )

    codes[tgt_me] = src_ref[...]
    pl.semaphore_wait(barrier, 4 * (Q - 1))

    def gather_hi(k):
        return copy(src_ref, codes.at[tgt_me], g_hi_send.at[k - 1], g_hi_recv.at[k - 1], hi_peer("tgt", k))

    def gather_lo(d, k):
        block = ((t_hi - d + Q) % Q) * Q + t_lo
        src = src_ref if isinstance(d, int) and d == 0 else codes.at[block]
        return copy(src, codes.at[block], g_lo_send.at[d, k - 1], g_lo_recv.at[d, k - 1], lo_peer("tgt", k))

    for k in range(1, Q):
        gather_hi(k).start()
    for k in range(1, Q):
        gather_lo(0, k).start()

    lane = lax.broadcasted_iota(jnp.int32, (B, D), 1)
    ones = jnp.where(lane < 3, 1.0, 0.0).astype(BF)
    sub16 = lax.broadcasted_iota(jnp.int32, (16, B), 0)

    src_t[pl.ds(D, D), :] = jnp.zeros((D, N), BF)
    tgt_t[pl.ds(D, D), :] = jnp.zeros((D, N), BF)
    tgt_one[:, pl.ds(D, D)] = jnp.ones((N, D), BF)

    def put_bias(rows_t, bias):
        hi = bias.astype(BF).astype(F32)
        rest = bias - hi
        mid = rest.astype(BF).astype(F32)
        low = rest - mid
        for k in range(NB):
            block = jnp.where(
                sub16 == 0, hi[k : k + 1, :],
                jnp.where(sub16 == 1, mid[k : k + 1, :], jnp.where(sub16 == 2, low[k : k + 1, :], 0.0)),
            )
            rows_t[pl.ds(D, 16), pl.ds(k * B, B)] = block.astype(BF)

    def turn(rows, rows_t, norm, at):
        turned = rows.astype(F32).T
        rows_t[pl.ds(0, D), pl.ds(pl.multiple_of(at * B, B), B)] = turned.astype(BF)
        norm[pl.ds(at, 1), :] = jnp.sum(turned * turned, axis=0, keepdims=True) * (0.5 / D)

    def turn_targets(k, carry):
        rows = tgt_ref[pl.ds(pl.multiple_of(k * B, B), B), :]
        tgt_one[pl.ds(pl.multiple_of(k * B, B), B), pl.ds(0, D)] = rows
        turn(rows, tgt_t, tgt_norm, k)
        return carry

    lax.fori_loop(0, NB, turn_targets, 0)
    put_bias(tgt_t, tgt_norm[...] * (-LOG2E / (EPS * SCALE)))

    def with_ones(rows):
        return jnp.concatenate([rows, ones], axis=1)

    def first_rows(at):
        rows = codes[at]
        turn(rows, src_t, src_norm, at)
        vec[0, pl.ds(at, 1), :] = lse_block(with_ones(rows), tgt_t[...])

    first_rows(tgt_me)
    for d in range(1, Q):
        gather_hi(d).wait_recv()
        for k in range(1, Q):
            gather_lo(d, k).start()

    def first_group(d, carry):
        hi = (t_hi - d + Q) % Q

        @pl.when(d > 0)
        def _():
            first_rows(hi * Q + t_lo)

        for k in range(1, Q):
            gather_lo(d, k).wait_recv()
            first_rows(hi * Q + (t_lo - k + Q) % Q)
        return carry

    lax.fori_loop(0, Q, first_group, 0)

    def combine(buf):
        high = jnp.maximum(jnp.maximum(buf[0], buf[1]), jnp.maximum(buf[2], buf[3]))
        total = jnp.exp2(buf[0] - high) + jnp.exp2(buf[1] - high)
        total = total + jnp.exp2(buf[2] - high) + jnp.exp2(buf[3] - high)
        return high + jnp.log2(total)

    def exchange(e, axis):
        hi, lo = (s_hi, s_lo) if axis == "src" else (t_hi, t_lo)
        for phase, (buf, mine, peer) in enumerate(((lo_buf, lo, lo_peer), (hi_buf, hi, hi_peer))):
            copies = [
                copy(
                    vec.at[2 * e + phase], buf.at[e, mine],
                    e_send.at[e, phase, k - 1], e_recv.at[e, phase, k - 1], peer(axis, k),
                )
                for k in range(1, Q)
            ]
            for c in copies:
                c.start()
            buf[e, mine] = vec[2 * e + phase]
            for c in copies:
                c.wait_recv()
            total = combine(buf[e])
            if phase == 0:
                vec[2 * e + 1] = total
            for c in copies:
                c.wait_send()
        return total

    def row_pass(e):
        def body(k, carry):
            vec[2 * e, pl.ds(k, 1), :] = lse_block(with_ones(codes[k]), tgt_t[...])
            return carry

        lax.fori_loop(0, NB, body, 0)

    def col_pass(e):
        def body(k, carry):
            rows = tgt_ref[pl.ds(pl.multiple_of(k * B, B), B), :]
            vec[2 * e, pl.ds(k, 1), :] = lse_block(with_ones(rows), src_t[...])
            return carry

        lax.fori_loop(0, NB, body, 0)

    slm = slm_ref[...] * LOG2E
    tlm = tlm_ref[...] * LOG2E
    back = EPS / LOG2E
    for it in range(2):
        if it > 0:
            row_pass(2 * it)
        src_log = slm - exchange(2 * it, "tgt")
        put_bias(src_t, src_log * (1.0 / SCALE))
        col_pass(2 * it + 1)
        tgt_log = tlm - exchange(2 * it + 1, "src")
        put_bias(tgt_t, tgt_log * (1.0 / SCALE))
    sd_ref[...] = src_log * back + src_norm[...]
    td_ref[...] = tgt_log * back + tgt_norm[...]

    def moments(at):
        u = jnp.dot(with_ones(codes[at]), tgt_t[...], preferred_element_type=F32)
        high = jnp.max(tile_high(u), axis=1, keepdims=True)
        w = jnp.exp2((u - high) * SCALE)
        w_hi = w.astype(BF)
        w_lo = (w - w_hi.astype(F32)).astype(BF)
        rhs = tgt_one[...]
        mom = jnp.dot(w_hi, rhs, preferred_element_type=F32) + jnp.dot(w_lo, rhs, preferred_element_type=F32)
        mass = mom[:, D:]
        return mom[:, :D] / mass, (high * SCALE + jnp.log2(mass)).T[:8, :]

    def send_lo(k, z):
        return copy(part.at[k % Q, z], got.at[k - 1, z], m_send.at[k - 1, z], m_recv.at[k - 1, z], lo_peer("tgt", k))

    def last_blocks(t, carry):
        k = (t // Q + 1) % Q
        z = t % Q
        mean, level = moments(z * Q + (t_lo + k) % Q)
        part[k, z, pl.ds(0, B), :] = mean
        part[k, z, pl.ds(B, 8), :] = level

        @pl.when(k > 0)
        def _():
            copy(
                part.at[k, z], got.at[jnp.maximum(k, 1) - 1, z], m_send.at[jnp.maximum(k, 1) - 1, z],
                m_recv.at[jnp.maximum(k, 1) - 1, z], {"tgt": t_hi * Q + (t_lo + jnp.maximum(k, 1)) % Q},
            ).start()

        return carry

    lax.fori_loop(0, NB, last_blocks, 0)

    def join(pieces):
        levels = [p[pl.ds(B, 8), :] for p in pieces]
        high = functools.reduce(jnp.maximum, levels)
        scaled = [jnp.exp2(v - high) for v in levels]
        total = functools.reduce(jnp.add, scaled)
        out = None
        for p, v in zip(pieces, scaled):
            share = jnp.broadcast_to((v / total)[:1, :], (B, B)).T
            term = p[pl.ds(0, B), :] * share
            out = term if out is None else out + term
        return out, high + jnp.log2(total)

    def send_hi(k):
        return copy(part2.at[k], got2.at[k - 1], r_send.at[k - 1], r_recv.at[k - 1], hi_peer("tgt", k))

    for k in (1, 2, 3, 0):
        z = (t_hi + k) % Q
        for j in range(1, Q):
            send_lo(j, z).wait_recv()
        mean, level = join([part.at[0, z]] + [got.at[j, z] for j in range(Q - 1)])
        part2[k, pl.ds(0, B), :] = mean
        part2[k, pl.ds(B, 8), :] = level
        if k > 0:
            send_hi(k).start()
    for k in range(1, Q):
        send_hi(k).wait_recv()
    mean, level = join([part2.at[0]] + [got2.at[j] for j in range(Q - 1)])
    map_ref[...] = mean

    for k in range(1, Q):
        gather_hi(k).wait_send()
        send_hi(k).wait_send()
        for d in range(Q):
            gather_lo(d, k).wait_send()
            send_lo(k, d).wait_send()


def shards(sources, targets, src_logmass, tgt_logmass):
    vmem = pl.BlockSpec(memory_space=pltpu.VMEM)
    dma = pltpu.SemaphoreType.DMA
    mapped, src_dual, tgt_dual = pl.pallas_call(
        kernel,
        out_shape=(
            jax.ShapeDtypeStruct((B, D), F32),
            jax.ShapeDtypeStruct((NB, B), F32),
            jax.ShapeDtypeStruct((NB, B), F32),
        ),
        in_specs=[vmem] * 4,
        out_specs=(vmem, vmem, vmem),
        scratch_shapes=[
            pltpu.VMEM((NB, B, D), BF),
            pltpu.VMEM((2 * D, N), BF),
            pltpu.VMEM((2 * D, N), BF),
            pltpu.VMEM((N, 2 * D), BF),
            pltpu.VMEM((NB, B), F32),
            pltpu.VMEM((NB, B), F32),
            pltpu.VMEM((8, NB, B), F32),
            pltpu.VMEM((4, Q, NB, B), F32),
            pltpu.VMEM((4, Q, NB, B), F32),
            pltpu.VMEM((Q, Q, B + 8, D), F32),
            pltpu.VMEM((Q - 1, Q, B + 8, D), F32),
            pltpu.VMEM((Q, B + 8, D), F32),
            pltpu.VMEM((Q - 1, B + 8, D), F32),
            dma((Q - 1,)), dma((Q - 1,)), dma((Q, Q - 1)), dma((Q, Q - 1)),
            dma((4, 2, Q - 1)), dma((4, 2, Q - 1)),
            dma((Q - 1, Q)), dma((Q - 1, Q)), dma((Q - 1,)), dma((Q - 1,)),
        ],
        compiler_params=pltpu.CompilerParams(
            collective_id=0, has_side_effects=True, vmem_limit_bytes=48 * 1024 * 1024
        ),
    )(sources, targets, src_logmass.reshape(NB, B), tgt_logmass.reshape(NB, B))
    return mapped, src_dual.reshape(N), tgt_dual.reshape(N)


def solution(mesh):
    return jax.shard_map(
        shards,
        mesh=mesh,
        in_specs=(P(("src", "tgt"), None), P("tgt", None), P("src"), P("tgt")),
        out_specs=(P(("src", "tgt"), None), P("src"), P("tgt")),
        check_vma=False,
    )
```

time: 707 us -> 114 us (0.16); the launches traced: 695 us -> 114 us
  blocking collectives: 443 us -> 0 us
  waiting for transfers between devices: 119 us -> 0 us
  Pallas kernels: 0 us -> 108 us
  matrix products: 81.8 us -> 0 us
  other arithmetic: 32.6 us -> 0 us
  between operations: 14.4 us -> 0.65 us
    pmax x5 -> x0, blocking collectives: 216 us -> none  [the longest x2 122 us: shards(): whole_col = lax.pmax(col_high, 'src')]
    psum x5 -> x0, blocking collectives: 186 us -> none  [the longest x2 86.8 us: shards(): col_sum = lax.psum(col_sum * jnp.exp(col_high - whole_col), 'src')]
    psum x1 -> x0, waiting for transfers between devices: 119 us -> none  [shards(): all_moment, all_mass = lax.psum((row_moment, row_mass), 'tgt')]
    pallas_call x0 -> x1, Pallas kernels: none -> 108 us  [shards(): pl.pallas_call(kernel, out_shape=(jax.ShapeDtypeStruct((B, D), F32), jax....]
    dot_general x28 -> x0, matrix products: 81.8 us -> none  [the longest x24 68.1 us: cost_tile(): lax.dot_general(src_block, targets, (((1,), (1,)), ((), ())), preferred_e...]
    all_gather x1 -> x0, blocking collectives: 40.6 us -> none  [shards(): src_codes = lax.all_gather(sources, 'tgt', axis=0, tiled=True)]
    reduce_sum x18 -> x0, other arithmetic: 29.7 us -> none  [the longest x8 22.2 us: col_step(): jnp.sum(jnp.exp(scores - new_high[None, :]), axis=0)]
  transfers between devices with their start and end apart: 1 -> 0, of which waited for: 1 -> 0; matrix products, arithmetic and copies ran while one was open for 0% -> 0% of each run, Pallas kernels for 0% -> 0%
where the time goes in v1:
time: 114 us
  Pallas kernels  108 us (95%)
  local copies, waits for them, and re-layouts  5.01 us (4%)
    pallas_call x1, Pallas kernels, shards(): pl.pallas_call(kernel, out_shape=(jax.ShapeDtypeStruct((B, D), F32), jax....  108 us
    unnamed x11, local copies, waits for them, and re-layouts  5.01 us

profile of v1, /device:TPU:1, one launch (start us, length us, event | category | flops | bytes accessed | tf_op | source)
XLA Modules:
  0.0 113.7 jit_solution(6247589093871232045)
XLA Ops:
  0.6 0.0 copy-start
  0.6 1.0 copy-done
  1.7 0.0 copy-start.1
  1.7 0.8 copy-done.1
  2.4 0.0 copy-start.2
  2.4 0.7 copy-done.2
  3.1 0.0 copy-start.3
  3.1 0.7 copy-done.3
  3.8 108.0 %shard_map.67 = (f32[128,128]{1,0:T(8,128)S(1)}, f32[16,128]{1,0:T(8,128)S(1)}, f32[16,128]{1,0:T(8,128)S(1)}) custom-call(bf16[128,128]{1,0:T(8,128)(2,1)S(1)} %copy-done.1, bf16[2048,128]{1,0:T(8,128)(2,1)S(1)} %copy-done, f32[16,128]{1,0:T(8,128)S(1)} %bitcast.4, f32[16,128]{1,0:T(8,128)S(1)} %bitcast.5), custom_call_target="tpu_custom_call" | custom-call | tf_op jit(solution)/shard_map/pallas_call | solution.py:283
  111.8 0.6 copy.10
  112.5 0.6 copy.11
  113.1 0.6 copy.12
Async XLA Ops:
  0.6 1.0 copy-start
  1.7 0.8 copy-start.1
  2.4 0.7 copy-start.2
  3.1 0.7 copy-start.3

commit v2 on v1

v2 whole, which is shorter than its diff:
```python
import functools
import math

import jax
import jax.numpy as jnp
from jax import lax
from jax.experimental import pallas as pl
from jax.experimental.pallas import tpu as pltpu
from jax.sharding import PartitionSpec as P

MESH = pl.DeviceIdType.MESH
EPS = 0.03125
LOG2E = math.log2(math.e)
B = 128
NB = 16
N = B * NB
D = 128
Q = 4
SCALE = LOG2E / (D * EPS)
BF = jnp.bfloat16
F32 = jnp.float32


GROUP = 16


def fold(x, op):
    x = op(x.reshape(x.shape[0] // GROUP, GROUP, x.shape[1]), axis=0)
    half = GROUP // 2
    return jnp.maximum(x[:half], x[half:]) if op is jnp.max else x[:half] + x[half:]


def lse_tile(rows, bias, rhs):
    high = None
    for q in range(NB):
        at = pl.ds(q * B, B)
        u = jnp.dot(jnp.concatenate([rows[at, :], bias[at, :]], axis=1), rhs, preferred_element_type=F32)
        new = fold(u, jnp.max)
        if high is not None:
            new = jnp.maximum(high, new)
        part = jnp.exp2((u.reshape(B // 8, 8, u.shape[1]) - new[None]) * SCALE).reshape(u.shape)
        part = fold(part, jnp.sum)
        total = part if high is None else total * jnp.exp2((high - new) * SCALE) + part
        high = new
    y = high * SCALE + jnp.log2(total)
    top = jnp.max(y, axis=0, keepdims=True)
    return top + jnp.log2(jnp.sum(jnp.exp2(y - top), axis=0, keepdims=True))


CHUNK = 256
UNROLL = 8


def moment_tile(rows, rows_t, bias, rhs):
    high = None
    for q in range(N // CHUNK):
        at = pl.ds(q * CHUNK, CHUNK)
        u = jnp.dot(jnp.concatenate([rows[at, :], bias[at, :]], axis=1), rhs, preferred_element_type=F32)
        new = jnp.max(fold(u, jnp.max), axis=0, keepdims=True)
        if high is not None:
            new = jnp.maximum(high, new)
        w = jnp.exp2((u - new) * SCALE)
        mass_part = fold(w, jnp.sum)
        w_hi = w.astype(BF)
        w_lo = (w - w_hi.astype(F32)).astype(BF)
        lhs = rows_t[:, at]
        part = jnp.dot(lhs, w_hi, preferred_element_type=F32) + jnp.dot(lhs, w_lo, preferred_element_type=F32)
        if high is None:
            total, mass = part, mass_part
        else:
            ratio = jnp.exp2((high - new) * SCALE)
            total, mass = total * ratio + part, mass * ratio + mass_part
        high = new
    mass = jnp.sum(mass, axis=0, keepdims=True)
    return total / mass, jnp.broadcast_to(high * SCALE + jnp.log2(mass), (8, rhs.shape[1]))


def kernel(
    src_ref, tgt_ref, slm_ref, tlm_ref, map_ref, sd_ref, td_ref,
    codes, src_t, tgt_t, src_bias, tgt_bias, src_norm, tgt_norm, vec, lo_buf, hi_buf,
    part, got, part2, got2,
    g_hi_send, g_hi_recv, g_lo_send, g_lo_recv,
    e_send, e_recv, m_send, m_recv, r_send, r_recv,
):
    src_me = lax.axis_index("src")
    tgt_me = lax.axis_index("tgt")
    s_hi, s_lo = src_me // Q, src_me % Q
    t_hi, t_lo = tgt_me // Q, tgt_me % Q

    def lo_peer(axis, k):
        hi, lo = (s_hi, s_lo) if axis == "src" else (t_hi, t_lo)
        return {axis: hi * Q + (lo + k) % Q}

    def hi_peer(axis, k):
        hi, lo = (s_hi, s_lo) if axis == "src" else (t_hi, t_lo)
        return {axis: ((hi + k) % Q) * Q + lo}

    barrier = pltpu.get_barrier_semaphore()
    for axis in ("tgt", "src"):
        for k in range(1, Q):
            pl.semaphore_signal(barrier, 1, device_id=lo_peer(axis, k), device_id_type=MESH)
            pl.semaphore_signal(barrier, 1, device_id=hi_peer(axis, k), device_id_type=MESH)

    def copy(src, dst, send, recv, peer):
        return pltpu.make_async_remote_copy(
            src_ref=src, dst_ref=dst, send_sem=send, recv_sem=recv, device_id=peer, device_id_type=MESH
        )

    def block_at(k):
        return pl.ds(pl.multiple_of(k * B, B), B)

    codes[block_at(tgt_me), :] = src_ref[...]
    pl.semaphore_wait(barrier, 4 * (Q - 1))

    def gather_hi(k):
        return copy(src_ref, codes.at[block_at(tgt_me), :], g_hi_send.at[k - 1], g_hi_recv.at[k - 1], hi_peer("tgt", k))

    def gather_lo(d, k):
        block = ((t_hi - d + Q) % Q) * Q + t_lo
        src = src_ref if isinstance(d, int) and d == 0 else codes.at[block_at(block), :]
        return copy(src, codes.at[block_at(block), :], g_lo_send.at[d, k - 1], g_lo_recv.at[d, k - 1], lo_peer("tgt", k))

    for k in range(1, Q):
        gather_hi(k).start()
    for k in range(1, Q):
        gather_lo(0, k).start()

    lane = lax.broadcasted_iota(jnp.int32, (B, B), 1)
    ones = jnp.ones((D, 2 * B), BF)

    def put_bias(out, bias):
        hi = bias.astype(BF).astype(F32)
        rest = bias - hi
        mid = rest.astype(BF).astype(F32)
        low = rest - mid
        turned = jnp.concatenate([hi, mid, low, jnp.zeros((B - 3 * NB, B), F32)], axis=0).T
        for k in range(NB):
            out[pl.ds(k * B, B), :] = jnp.where(lane % NB == k, turned, 0.0).astype(BF)

    def turn(rows, rows_t, norm, at):
        turned = rows.astype(F32).T
        rows_t[:, block_at(at)] = turned.astype(BF)
        norm[pl.ds(at, 1), :] = jnp.sum(turned * turned, axis=0, keepdims=True) * (0.5 / D)

    def under(rows_t, first, second):
        pair = jnp.concatenate([rows_t[:, block_at(first)], rows_t[:, block_at(second)]], axis=1)
        return jnp.concatenate([pair, ones], axis=0)

    for k in range(NB):
        turn(tgt_ref[pl.ds(k * B, B), :], tgt_t, tgt_norm, k)
    put_bias(tgt_bias, tgt_norm[...] * (-LOG2E / (EPS * SCALE)))

    def take(at):
        turn(codes[block_at(at), :], src_t, src_norm, at)

    def first_pair(first, second):
        total = lse_tile(tgt_ref, tgt_bias, under(src_t, first, second))
        vec[0, pl.ds(first, 1), :] = total[:, :B]
        vec[0, pl.ds(second, 1), :] = total[:, B:]

    for d in range(1, Q):
        gather_hi(d).wait_recv()
        for k in range(1, Q):
            gather_lo(d, k).start()

    def first_group(d, carry):
        hi = (t_hi - d + Q) % Q
        at = [hi * Q + (t_lo - k + Q) % Q for k in range(Q)]
        take(at[0])
        gather_lo(d, 1).wait_recv()
        take(at[1])
        first_pair(at[0], at[1])
        gather_lo(d, 2).wait_recv()
        take(at[2])
        gather_lo(d, 3).wait_recv()
        take(at[3])
        first_pair(at[2], at[3])
        return carry

    lax.fori_loop(0, Q, first_group, 0)

    def combine(buf):
        high = jnp.maximum(jnp.maximum(buf[0], buf[1]), jnp.maximum(buf[2], buf[3]))
        total = jnp.exp2(buf[0] - high) + jnp.exp2(buf[1] - high)
        total = total + jnp.exp2(buf[2] - high) + jnp.exp2(buf[3] - high)
        return high + jnp.log2(total)

    def exchange(e, axis):
        hi, lo = (s_hi, s_lo) if axis == "src" else (t_hi, t_lo)
        for phase, (buf, mine, peer) in enumerate(((lo_buf, lo, lo_peer), (hi_buf, hi, hi_peer))):
            copies = [
                copy(
                    vec.at[2 * e + phase], buf.at[e, mine],
                    e_send.at[e, phase, k - 1], e_recv.at[e, phase, k - 1], peer(axis, k),
                )
                for k in range(1, Q)
            ]
            for c in copies:
                c.start()
            buf[e, mine] = vec[2 * e + phase]
            for c in copies:
                c.wait_recv()
            total = combine(buf[e])
            if phase == 0:
                vec[2 * e + 1] = total
            for c in copies:
                c.wait_send()
        return total

    def whole_pass(e, rows, bias, rows_t):
        def body(k, carry):
            total = lse_tile(rows, bias, under(rows_t, 2 * k, 2 * k + 1))
            vec[2 * e, pl.ds(2 * k, 1), :] = total[:, :B]
            vec[2 * e, pl.ds(2 * k + 1, 1), :] = total[:, B:]
            return carry

        lax.fori_loop(0, NB // 2, body, 0, unroll=UNROLL)

    slm = slm_ref[...] * LOG2E
    tlm = tlm_ref[...] * LOG2E
    back = EPS / LOG2E
    for it in range(2):
        if it > 0:
            whole_pass(2 * it, tgt_ref, tgt_bias, src_t)
        src_log = slm - exchange(2 * it, "tgt")
        put_bias(src_bias, src_log * (1.0 / SCALE))
        whole_pass(2 * it + 1, codes, src_bias, tgt_t)
        tgt_log = tlm - exchange(2 * it + 1, "src")
        put_bias(tgt_bias, tgt_log * (1.0 / SCALE))
    sd_ref[...] = src_log * back + src_norm[...]
    td_ref[...] = tgt_log * back + tgt_norm[...]

    def send_lo(k, z):
        return copy(part.at[k % Q, z], got.at[k - 1, z], m_send.at[k - 1, z], m_recv.at[k - 1, z], lo_peer("tgt", k))

    def last_group(t, carry):
        k = (t + 1) % Q
        x = (t_lo + k) % Q
        for z in range(0, Q, 2):
            mean, level = moment_tile(tgt_ref, tgt_t, tgt_bias, under(src_t, z * Q + x, (z + 1) * Q + x))
            for j in range(2):
                part[k, z + j, pl.ds(0, B), :] = mean[:, j * B : (j + 1) * B]
                part[k, z + j, pl.ds(B, 8), :] = level[:, j * B : (j + 1) * B]

        @pl.when(k > 0)
        def _():
            near = jnp.maximum(k, 1)
            for z in range(Q):
                copy(
                    part.at[k, z], got.at[near - 1, z], m_send.at[near - 1, z],
                    m_recv.at[near - 1, z], {"tgt": t_hi * Q + (t_lo + near) % Q},
                ).start()

        return carry

    lax.fori_loop(0, Q, last_group, 0)

    def join(pieces):
        levels = [p[pl.ds(B, 8), :] for p in pieces]
        high = functools.reduce(jnp.maximum, levels)
        scaled = [jnp.exp2(v - high) for v in levels]
        total = functools.reduce(jnp.add, scaled)
        out = None
        for p, v in zip(pieces, scaled):
            term = p[pl.ds(0, B), :] * (v / total)[:1, :]
            out = term if out is None else out + term
        return out, high + jnp.log2(total)

    def send_hi(k):
        return copy(part2.at[k], got2.at[k - 1], r_send.at[k - 1], r_recv.at[k - 1], hi_peer("tgt", k))

    for k in (1, 2, 3, 0):
        z = (t_hi + k) % Q
        for j in range(1, Q):
            send_lo(j, z).wait_recv()
        mean, level = join([part.at[0, z]] + [got.at[j, z] for j in range(Q - 1)])
        part2[k, pl.ds(0, B), :] = mean
        part2[k, pl.ds(B, 8), :] = level
        if k > 0:
            send_hi(k).start()
    for k in range(1, Q):
        send_hi(k).wait_recv()
    mean, level = join([part2.at[0]] + [got2.at[j] for j in range(Q - 1)])
    map_ref[...] = mean.T

    for k in range(1, Q):
        gather_hi(k).wait_send()
        send_hi(k).wait_send()
        for d in range(Q):
            gather_lo(d, k).wait_send()
            send_lo(k, d).wait_send()


def shards(sources, targets, src_logmass, tgt_logmass):
    vmem = pl.BlockSpec(memory_space=pltpu.VMEM)
    dma = pltpu.SemaphoreType.DMA
    mapped, src_dual, tgt_dual = pl.pallas_call(
        kernel,
        out_shape=(
            jax.ShapeDtypeStruct((B, D), F32),
            jax.ShapeDtypeStruct((NB, B), F32),
            jax.ShapeDtypeStruct((NB, B), F32),
        ),
        in_specs=[vmem] * 4,
        out_specs=(vmem, vmem, vmem),
        scratch_shapes=[
            pltpu.VMEM((N, D), BF),
            pltpu.VMEM((D, N), BF),
            pltpu.VMEM((D, N), BF),
            pltpu.VMEM((N, B), BF),
            pltpu.VMEM((N, B), BF),
            pltpu.VMEM((NB, B), F32),
            pltpu.VMEM((NB, B), F32),
            pltpu.VMEM((8, NB, B), F32),
            pltpu.VMEM((4, Q, NB, B), F32),
            pltpu.VMEM((4, Q, NB, B), F32),
            pltpu.VMEM((Q, Q, B + 8, D), F32),
            pltpu.VMEM((Q - 1, Q, B + 8, D), F32),
            pltpu.VMEM((Q, B + 8, D), F32),
            pltpu.VMEM((Q - 1, B + 8, D), F32),
            dma((Q - 1,)), dma((Q - 1,)), dma((Q, Q - 1)), dma((Q, Q - 1)),
            dma((4, 2, Q - 1)), dma((4, 2, Q - 1)),
            dma((Q - 1, Q)), dma((Q - 1, Q)), dma((Q - 1,)), dma((Q - 1,)),
        ],
        compiler_params=pltpu.CompilerParams(
            collective_id=0, has_side_effects=True, vmem_limit_bytes=48 * 1024 * 1024
        ),
    )(sources, targets, src_logmass.reshape(NB, B), tgt_logmass.reshape(NB, B))
    return mapped, src_dual.reshape(N), tgt_dual.reshape(N)


def solution(mesh):
    return jax.shard_map(
        shards,
        mesh=mesh,
        in_specs=(P(("src", "tgt"), None), P("tgt", None), P("src"), P("tgt")),
        out_specs=(P(("src", "tgt"), None), P("src"), P("tgt")),
        check_vma=False,
    )
```

time: 114 us -> 94.1 us (0.83); the launches traced: 114 us -> 92.3 us
  Pallas kernels: 108 us -> 86.7 us
    pallas_call x1, Pallas kernels: 108 us -> 86.7 us  [shards(): pl.pallas_call(kernel, out_shape=(jax.ShapeDtypeStruct((B, D), F32), jax....]
where the time goes in v2:
time: 94.1 us; the launch traced here: 92.3 us
  Pallas kernels  86.7 us (92%)
  local copies, waits for them, and re-layouts  5.01 us (5%)
    pallas_call x1, Pallas kernels, shards(): pl.pallas_call(kernel, out_shape=(jax.ShapeDtypeStruct((B, D), F32), jax....  86.7 us
    unnamed x11, local copies, waits for them, and re-layouts  5.01 us

profile of v2, /device:TPU:1, one launch (start us, length us, event | category | flops | bytes accessed | tf_op | source)
XLA Modules:
  0.0 92.3 jit_solution(17252496064451475376)
XLA Ops:
  0.6 0.0 copy-start
  0.6 1.0 %copy-done = bf16[2048,128]{1,0:T(8,128)(2,1)S(1)} copy-done((bf16[2048,128]{1,0:T(8,128)(2,1)S(1)}, bf16[2048,128]{1,0:T(8,128)(2,1)}, u32[]{:S(2)}) %copy-start) | copy-done | bytes 524312
  1.7 0.0 copy-start.1
  1.7 0.8 copy-done.1
  2.4 0.0 copy-start.2
  2.4 0.7 copy-done.2
  3.1 0.0 copy-start.3
  3.1 0.7 copy-done.3
  3.8 86.7 %shard_map.67 = (f32[128,128]{1,0:T(8,128)S(1)}, f32[16,128]{1,0:T(8,128)S(1)}, f32[16,128]{1,0:T(8,128)S(1)}) custom-call(bf16[128,128]{1,0:T(8,128)(2,1)S(1)} %copy-done.1, bf16[2048,128]{1,0:T(8,128)(2,1)S(1)} %copy-done, f32[16,128]{1,0:T(8,128)S(1)} %bitcast.4, f32[16,128]{1,0:T(8,128)S(1)} %bitcast.5), custom_call_target="tpu_custom_call" | custom-call | tf_op jit(solution)/shard_map/pallas_call | solution.py:297
  90.5 0.6 copy.10
  91.1 0.6 copy.11
  91.7 0.6 copy.12
Async XLA Ops:
  0.6 1.0 %copy-start = (bf16[2048,128]{1,0:T(8,128)(2,1)S(1)}, bf16[2048,128]{1,0:T(8,128)(2,1)}, u32[]{:S(2)}) copy-start(bf16[2048,128]{1,0:T(8,128)(2,1)} %tgt_ref.1) | copy-start | bytes 1572868
  1.7 0.8 copy-start.1
  2.4 0.7 copy-start.2
  3.1 0.7 copy-start.3

commit v3 on v2

--- a/solution.py
+++ b/solution.py
@@ -21,6 +21,7 @@
 F32 = jnp.float32
 
 
+FILL = 7250
 GROUP = 16
 
 
@@ -48,7 +49,7 @@
 
 
 CHUNK = 256
-UNROLL = 8
+UNROLL = 4
 
 
 def moment_tile(rows, rows_t, bias, rhs):
@@ -76,9 +77,9 @@
 
 
 def kernel(
-    src_ref, tgt_ref, slm_ref, tlm_ref, map_ref, sd_ref, td_ref,
-    codes, src_t, tgt_t, src_bias, tgt_bias, src_norm, tgt_norm, vec, lo_buf, hi_buf,
-    part, got, part2, got2,
+    src_hbm, tgt_hbm, slm_hbm, tlm_hbm, map_ref, sd_ref, td_ref,
+    rows, rows_t, bias, logmass, norm, dual, vec, inbox,
+    part, got, part2, got2, in_sem,
     g_hi_send, g_hi_recv, g_lo_send, g_lo_recv,
     e_send, e_recv, m_send, m_recv, r_send, r_recv,
 ):
@@ -95,35 +96,39 @@
         hi, lo = (s_hi, s_lo) if axis == "src" else (t_hi, t_lo)
         return {axis: ((hi + k) % Q) * Q + lo}
 
+    codes, src_t, src_norm = rows.at[0], rows_t.at[0], norm.at[0]
+    tgt_ref, tgt_t, tgt_norm, tgt_bias = rows.at[1], rows_t.at[1], norm.at[1], bias.at[1]
+
+    def block_at(k):
+        return pl.ds(pl.multiple_of(k * B, B), B)
+
+    fetches = [
+        pltpu.make_async_copy(src, dst, in_sem.at[i])
+        for i, (src, dst) in enumerate((
+            (src_hbm, codes.at[block_at(tgt_me), :]), (tgt_hbm, tgt_ref), (slm_hbm, logmass.at[0]), (tlm_hbm, logmass.at[1]),
+        ))
+    ]
+    for f in fetches:
+        f.start()
+
     barrier = pltpu.get_barrier_semaphore()
-    for axis in ("tgt", "src"):
-        for k in range(1, Q):
-            pl.semaphore_signal(barrier, 1, device_id=lo_peer(axis, k), device_id_type=MESH)
-            pl.semaphore_signal(barrier, 1, device_id=hi_peer(axis, k), device_id_type=MESH)
+    for k in range(1, NB):
+        for axis, me in (("tgt", tgt_me), ("src", src_me)):
+            pl.semaphore_signal(barrier, 1, device_id={axis: (me + k) % NB}, device_id_type=MESH)
 
     def copy(src, dst, send, recv, peer):
         return pltpu.make_async_remote_copy(
             src_ref=src, dst_ref=dst, send_sem=send, recv_sem=recv, device_id=peer, device_id_type=MESH
         )
 
-    def block_at(k):
-        return pl.ds(pl.multiple_of(k * B, B), B)
-
-    codes[block_at(tgt_me), :] = src_ref[...]
-    pl.semaphore_wait(barrier, 4 * (Q - 1))
-
     def gather_hi(k):
-        return copy(src_ref, codes.at[block_at(tgt_me), :], g_hi_send.at[k - 1], g_hi_recv.at[k - 1], hi_peer("tgt", k))
+        own = codes.at[block_at(tgt_me), :]
+        return copy(own, own, g_hi_send.at[k - 1], g_hi_recv.at[k - 1], hi_peer("tgt", k))
 
     def gather_lo(d, k):
         block = ((t_hi - d + Q) % Q) * Q + t_lo
-        src = src_ref if isinstance(d, int) and d == 0 else codes.at[block_at(block), :]
-        return copy(src, codes.at[block_at(block), :], g_lo_send.at[d, k - 1], g_lo_recv.at[d, k - 1], lo_peer("tgt", k))
-
-    for k in range(1, Q):
-        gather_hi(k).start()
-    for k in range(1, Q):
-        gather_lo(0, k).start()
+        rows = codes.at[block_at(block), :]
+        return copy(rows, rows, g_lo_send.at[d, k - 1], g_lo_recv.at[d, k - 1], lo_peer("tgt", k))
 
     lane = lax.broadcasted_iota(jnp.int32, (B, B), 1)
     ones = jnp.ones((D, 2 * B), BF)
@@ -146,6 +151,15 @@
         pair = jnp.concatenate([rows_t[:, block_at(first)], rows_t[:, block_at(second)]], axis=1)
         return jnp.concatenate([pair, ones], axis=0)
 
+    fetches[0].wait()
+    pl.semaphore_wait(barrier, 2 * (NB - 1))
+    for k in range(1, Q):
+        gather_hi(k).start()
+    for k in range(1, Q):
+        gather_lo(0, k).start()
+
+    for f in fetches[1:]:
+        f.wait()
     for k in range(NB):
         turn(tgt_ref[pl.ds(k * B, B), :], tgt_t, tgt_norm, k)
     put_bias(tgt_bias, tgt_norm[...] * (-LOG2E / (EPS * SCALE)))
@@ -155,8 +169,8 @@
 
     def first_pair(first, second):
         total = lse_tile(tgt_ref, tgt_bias, under(src_t, first, second))
-        vec[0, pl.ds(first, 1), :] = total[:, :B]
-        vec[0, pl.ds(second, 1), :] = total[:, B:]
+        vec[0, first // 8, pl.ds(first % 8, 1), :] = total[:, :B]
+        vec[0, second // 8, pl.ds(second % 8, 1), :] = total[:, B:]
 
     for d in range(1, Q):
         gather_hi(d).wait_recv()
@@ -179,56 +193,56 @@
 
     lax.fori_loop(0, Q, first_group, 0)
 
-    def combine(buf):
-        high = jnp.maximum(jnp.maximum(buf[0], buf[1]), jnp.maximum(buf[2], buf[3]))
-        total = jnp.exp2(buf[0] - high) + jnp.exp2(buf[1] - high)
-        total = total + jnp.exp2(buf[2] - high) + jnp.exp2(buf[3] - high)
-        return high + jnp.log2(total)
-
-    def exchange(e, axis):
-        hi, lo = (s_hi, s_lo) if axis == "src" else (t_hi, t_lo)
-        for phase, (buf, mine, peer) in enumerate(((lo_buf, lo, lo_peer), (hi_buf, hi, hi_peer))):
-            copies = [
-                copy(
-                    vec.at[2 * e + phase], buf.at[e, mine],
-                    e_send.at[e, phase, k - 1], e_recv.at[e, phase, k - 1], peer(axis, k),
-                )
-                for k in range(1, Q)
-            ]
-            for c in copies:
-                c.start()
-            buf[e, mine] = vec[2 * e + phase]
-            for c in copies:
-                c.wait_recv()
-            total = combine(buf[e])
-            if phase == 0:
-                vec[2 * e + 1] = total
-            for c in copies:
-                c.wait_send()
-        return total
-
-    def whole_pass(e, rows, bias, rows_t):
-        def body(k, carry):
-            total = lse_tile(rows, bias, under(rows_t, 2 * k, 2 * k + 1))
-            vec[2 * e, pl.ds(2 * k, 1), :] = total[:, :B]
-            vec[2 * e, pl.ds(2 * k + 1, 1), :] = total[:, B:]
+    def message(e, h, k):
+        odd = e % 2
+        peer = ((src_me + odd * k) % NB, (tgt_me + (1 - odd) * k) % NB)
+        mine = odd * src_me + (1 - odd) * tgt_me
+        return copy(vec.at[e, h], inbox.at[e, h, mine], e_send.at[e, h], e_recv.at[e, h], peer)
+
+    def send_half(e, h):
+        for k in range(1, NB):
+            message(e, h, k).start()
+        inbox[e, h, (e % 2) * src_me + (1 - e % 2) * tgt_me] = vec[e, h]
+
+    def all_bytes(e, h, sem):
+        others = inbox.at[e, h, pl.ds(0, NB - 1)]
+        return pltpu.make_async_copy(others, others, sem.at[e, h])
+
+    def receive(e):
+        for h in range(2):
+            all_bytes(e, h, e_recv).wait()
+        pieces = [inbox[e, :, k].reshape(NB, B) for k in range(NB)]
+        high = functools.reduce(jnp.maximum, pieces)
+        level = high + jnp.log2(functools.reduce(jnp.add, [jnp.exp2(p - high) for p in pieces]))
+        side = e % 2
+        log = logmass[side] * LOG2E - level
+        put_bias(bias.at[side], log * (1.0 / SCALE))
+        dual[side] = log * (EPS / LOG2E) + norm[side]
+
+    def whole_pass(e, carry):
+        receive(e - 1)
+        side = (e - 1) % 2
+
+        def half(h, carry):
+            def body(k, carry):
+                at = h * (NB // 4) + k
+                total = lse_tile(rows.at[side], bias.at[side], under(rows_t.at[1 - side], 2 * at, 2 * at + 1))
+                vec[e, h, pl.ds(2 * k, 1), :] = total[:, :B]
+                vec[e, h, pl.ds(2 * k + 1, 1), :] = total[:, B:]
+                return carry
+
+            lax.fori_loop(0, NB // 4, body, 0, unroll=UNROLL)
+            send_half(e, h)
             return carry
 
-        lax.fori_loop(0, NB // 2, body, 0, unroll=UNROLL)
-
-    slm = slm_ref[...] * LOG2E
-    tlm = tlm_ref[...] * LOG2E
-    back = EPS / LOG2E
-    for it in range(2):
-        if it > 0:
-            whole_pass(2 * it, tgt_ref, tgt_bias, src_t)
-        src_log = slm - exchange(2 * it, "tgt")
-        put_bias(src_bias, src_log * (1.0 / SCALE))
-        whole_pass(2 * it + 1, codes, src_bias, tgt_t)
-        tgt_log = tlm - exchange(2 * it + 1, "src")
-        put_bias(tgt_bias, tgt_log * (1.0 / SCALE))
-    sd_ref[...] = src_log * back + src_norm[...]
-    td_ref[...] = tgt_log * back + tgt_norm[...]
+        return lax.fori_loop(0, 2, half, carry)
+
+    send_half(0, 0)
+    send_half(0, 1)
+    lax.fori_loop(1, 4, whole_pass, 0)
+    receive(3)
+    sd_ref[...] = dual[0]
+    td_ref[...] = dual[1]
 
     def send_lo(k, z):
         return copy(part.at[k % Q, z], got.at[k - 1, z], m_send.at[k - 1, z], m_recv.at[k - 1, z], lo_peer("tgt", k))
@@ -236,20 +250,20 @@
     def last_group(t, carry):
         k = (t + 1) % Q
         x = (t_lo + k) % Q
+        near = jnp.maximum(k, 1)
         for z in range(0, Q, 2):
             mean, level = moment_tile(tgt_ref, tgt_t, tgt_bias, under(src_t, z * Q + x, (z + 1) * Q + x))
             for j in range(2):
                 part[k, z + j, pl.ds(0, B), :] = mean[:, j * B : (j + 1) * B]
                 part[k, z + j, pl.ds(B, 8), :] = level[:, j * B : (j + 1) * B]
 
-        @pl.when(k > 0)
-        def _():
-            near = jnp.maximum(k, 1)
-            for z in range(Q):
-                copy(
-                    part.at[k, z], got.at[near - 1, z], m_send.at[near - 1, z],
-                    m_recv.at[near - 1, z], {"tgt": t_hi * Q + (t_lo + near) % Q},
-                ).start()
+            @pl.when(k > 0)
+            def _():
+                for j in range(z, z + 2):
+                    copy(
+                        part.at[k, j], got.at[near - 1, j], m_send.at[near - 1, j],
+                        m_recv.at[near - 1, j], {"tgt": t_hi * Q + (t_lo + near) % Q},
+                    ).start()
 
         return carry
 
@@ -289,6 +303,9 @@
         for d in range(Q):
             gather_lo(d, k).wait_send()
             send_lo(k, d).wait_send()
+    for e in range(4):
+        for h in range(2):
+            all_bytes(e, h, e_send).wait()
 
 
 def shards(sources, targets, src_logmass, tgt_logmass):
@@ -301,29 +318,28 @@
             jax.ShapeDtypeStruct((NB, B), F32),
             jax.ShapeDtypeStruct((NB, B), F32),
         ),
-        in_specs=[vmem] * 4,
+        in_specs=[pl.BlockSpec(memory_space=pltpu.HBM)] * 4,
         out_specs=(vmem, vmem, vmem),
         scratch_shapes=[
-            pltpu.VMEM((N, D), BF),
-            pltpu.VMEM((D, N), BF),
-            pltpu.VMEM((D, N), BF),
-            pltpu.VMEM((N, B), BF),
-            pltpu.VMEM((N, B), BF),
-            pltpu.VMEM((NB, B), F32),
-            pltpu.VMEM((NB, B), F32),
-            pltpu.VMEM((8, NB, B), F32),
-            pltpu.VMEM((4, Q, NB, B), F32),
-            pltpu.VMEM((4, Q, NB, B), F32),
+            pltpu.VMEM((2, N, D), BF),
+            pltpu.VMEM((2, D, N), BF),
+            pltpu.VMEM((2, N, B), BF),
+            pltpu.VMEM((FILL, NB, B), F32),
+            pltpu.VMEM((2, NB, B), F32),
+            pltpu.VMEM((2, NB, B), F32),
+            pltpu.VMEM((4, 2, NB // 2, B), F32),
+            pltpu.VMEM((4, 2, NB, NB // 2, B), F32),
             pltpu.VMEM((Q, Q, B + 8, D), F32),
             pltpu.VMEM((Q - 1, Q, B + 8, D), F32),
             pltpu.VMEM((Q, B + 8, D), F32),
             pltpu.VMEM((Q - 1, B + 8, D), F32),
+            dma((4,)),
             dma((Q - 1,)), dma((Q - 1,)), dma((Q, Q - 1)), dma((Q, Q - 1)),
-            dma((4, 2, Q - 1)), dma((4, 2, Q - 1)),
+            dma((4, 2)), dma((4, 2)),
             dma((Q - 1, Q)), dma((Q - 1, Q)), dma((Q - 1,)), dma((Q - 1,)),
         ],
         compiler_params=pltpu.CompilerParams(
-            collective_id=0, has_side_effects=True, vmem_limit_bytes=48 * 1024 * 1024
+            collective_id=0, has_side_effects=True, vmem_limit_bytes=64 * 1024 * 1024
         ),
     )(sources, targets, src_logmass.reshape(NB, B), tgt_logmass.reshape(NB, B))
     return mapped, src_dual.reshape(N), tgt_dual.reshape(N)

time: 94.1 us -> 87.9 us (0.934)
  Pallas kernels: 86.7 us -> 83.5 us
  local copies, waits for them, and re-layouts: 5.01 us -> 2.78 us
    pallas_call x1, Pallas kernels: 86.7 us -> 83.5 us  [shards(): pl.pallas_call(kernel, out_shape=(jax.ShapeDtypeStruct((B, D), F32), jax....]
    unnamed x11 -> x7, local copies, waits for them, and re-layouts: 5.01 us -> 2.78 us
where the time goes in v3:
time: 87.9 us; the launch traced here: 87 us
  Pallas kernels  83.5 us (95%)
  local copies, waits for them, and re-layouts  2.78 us (3%)
    pallas_call x1, Pallas kernels, shards(): pl.pallas_call(kernel, out_shape=(jax.ShapeDtypeStruct((B, D), F32), jax....  83.5 us
    unnamed x7, local copies, waits for them, and re-layouts  2.78 us

profile of v3, /device:TPU:1, one launch (start us, length us, event | category | flops | bytes accessed | tf_op | source)
XLA Modules:
  0.0 87.0 jit_solution(10420440731068441643)
XLA Ops:
  0.6 83.5 %shard_map.67 = (f32[128,128]{1,0:T(8,128)}, f32[16,128]{1,0:T(8,128)}, f32[16,128]{1,0:T(8,128)}) custom-call(bf16[128,128]{1,0:T(8,128)(2,1)} %src_hbm.1, bf16[2048,128]{1,0:T(8,128)(2,1)} %tgt_hbm.1, f32[16,128]{1,0:T(8,128)} %bitcast.4, f32[16,128]{1,0:T(8,128)} %bitcast.5), custom_call_target="tpu_custom_call" | custom-call | tf_op jit(solution)/shard_map/pallas_call | solution.py:314
  84.2 0.0 copy-start.1
  84.2 1.5 %copy.10 = f32[128,128]{1,0:T(8,128)} copy(f32[128,128]{1,0:T(8,128)} %get-tuple-element.12) | data formatting | bytes 131072
  85.7 0.0 copy-done.1
  85.7 0.0 copy-start
  85.7 0.6 copy.11
  86.3 0.1 copy-done
  86.4 0.6 copy.12
Async XLA Ops:
  84.2 1.5 %copy-start.1 = (f32[16,128]{1,0:T(8,128)S(1)}, f32[16,128]{1,0:T(8,128)}, u32[]{:S(2)}) copy-start(f32[16,128]{1,0:T(8,128)} %get-tuple-element.7) | copy-start | bytes 24580
  85.7 0.7 copy-start

commit v4 on v3

--- a/solution.py
+++ b/solution.py
@@ -21,7 +21,7 @@
 F32 = jnp.float32
 
 
-FILL = 7250
+FILL = 6880
 GROUP = 16
 
 
@@ -52,36 +52,29 @@
 UNROLL = 4
 
 
-def moment_tile(rows, rows_t, bias, rhs):
-    high = None
+def moment_step(rows, rows_t, bias, rhs, high, mass, total):
     for q in range(N // CHUNK):
         at = pl.ds(q * CHUNK, CHUNK)
         u = jnp.dot(jnp.concatenate([rows[at, :], bias[at, :]], axis=1), rhs, preferred_element_type=F32)
-        new = jnp.max(fold(u, jnp.max), axis=0, keepdims=True)
-        if high is not None:
-            new = jnp.maximum(high, new)
+        new = jnp.maximum(high, jnp.max(fold(u, jnp.max), axis=0, keepdims=True))
         w = jnp.exp2((u - new) * SCALE)
-        mass_part = fold(w, jnp.sum)
         w_hi = w.astype(BF)
         w_lo = (w - w_hi.astype(F32)).astype(BF)
         lhs = rows_t[:, at]
+        ratio = jnp.exp2((high - new) * SCALE)
+        mass = mass * ratio + fold(w, jnp.sum)
         part = jnp.dot(lhs, w_hi, preferred_element_type=F32) + jnp.dot(lhs, w_lo, preferred_element_type=F32)
-        if high is None:
-            total, mass = part, mass_part
-        else:
-            ratio = jnp.exp2((high - new) * SCALE)
-            total, mass = total * ratio + part, mass * ratio + mass_part
+        total = total * ratio + part
         high = new
-    mass = jnp.sum(mass, axis=0, keepdims=True)
-    return total / mass, jnp.broadcast_to(high * SCALE + jnp.log2(mass), (8, rhs.shape[1]))
+    return high, mass, total
 
 
 def kernel(
     src_hbm, tgt_hbm, slm_hbm, tlm_hbm, map_ref, sd_ref, td_ref,
     rows, rows_t, bias, logmass, norm, dual, vec, inbox,
-    part, got, part2, got2, in_sem,
+    moment, mass, high, far_bias, part, got, in_sem,
     g_hi_send, g_hi_recv, g_lo_send, g_lo_recv,
-    e_send, e_recv, m_send, m_recv, r_send, r_recv,
+    e_send, e_recv, x_send, x_recv, f_send, f_recv, b_send, b_recv, r_send, r_recv,
 ):
     src_me = lax.axis_index("src")
     tgt_me = lax.axis_index("tgt")
@@ -219,8 +212,23 @@
         put_bias(bias.at[side], log * (1.0 / SCALE))
         dual[side] = log * (EPS / LOG2E) + norm[side]
 
+    half_rows = pl.ds(pl.multiple_of(src_me % 2 * (N // 2), N // 2), N // 2)
+
+    def spread(k):
+        return copy(rows.at[1, half_rows, :], rows.at[1 + k, half_rows, :], x_send.at[k - 1], x_recv.at[k - 1], lo_peer("tgt", k))
+
+    def hand_over(k):
+        there = rows.at[1 + k, half_rows, :]
+        return copy(there, there, f_send.at[k - 1], f_recv.at[k - 1], {"src": src_me + 1 - 2 * (src_me % 2)})
+
     def whole_pass(e, carry):
         receive(e - 1)
+
+        @pl.when(e == 1)
+        def _():
+            for k in range(1, Q):
+                spread(k).start()
+
         side = (e - 1) % 2
 
         def half(h, carry):
@@ -235,74 +243,117 @@
             send_half(e, h)
             return carry
 
-        return lax.fori_loop(0, 2, half, carry)
+        lax.fori_loop(0, 2, half, 0)
+
+        @pl.when(e == 2)
+        def _():
+            for k in range(1, Q):
+                spread(k).wait_recv()
+                hand_over(k).start()
+
+        return carry
 
     send_half(0, 0)
     send_half(0, 1)
     lax.fori_loop(1, 4, whole_pass, 0)
+    for k in range(1, Q):
+        hand_over(k).wait_recv()
+
+    def turn_far(j, carry):
+        for k in range(NB):
+            rows_t[j, :, pl.ds(k * B, B)] = rows[j, pl.ds(k * B, B), :].astype(F32).T.astype(BF)
+        return carry
+
+    lax.fori_loop(2, 2 + Q - 1, turn_far, 0)
     receive(3)
     sd_ref[...] = dual[0]
     td_ref[...] = dual[1]
 
-    def send_lo(k, z):
-        return copy(part.at[k % Q, z], got.at[k - 1, z], m_send.at[k - 1, z], m_recv.at[k - 1, z], lo_peer("tgt", k))
-
-    def last_group(t, carry):
-        k = (t + 1) % Q
-        x = (t_lo + k) % Q
-        near = jnp.maximum(k, 1)
-        for z in range(0, Q, 2):
-            mean, level = moment_tile(tgt_ref, tgt_t, tgt_bias, under(src_t, z * Q + x, (z + 1) * Q + x))
-            for j in range(2):
-                part[k, z + j, pl.ds(0, B), :] = mean[:, j * B : (j + 1) * B]
-                part[k, z + j, pl.ds(B, 8), :] = level[:, j * B : (j + 1) * B]
-
-            @pl.when(k > 0)
-            def _():
-                for j in range(z, z + 2):
-                    copy(
-                        part.at[k, j], got.at[near - 1, j], m_send.at[near - 1, j],
-                        m_recv.at[near - 1, j], {"tgt": t_hi * Q + (t_lo + near) % Q},
-                    ).start()
-
+    def send_bias(k):
+        return copy(far_bias.at[0], far_bias.at[k], b_send.at[k - 1], b_recv.at[k - 1], lo_peer("tgt", k))
+
+    far_bias[0] = (dual[1] - tgt_norm[...]) * (LOG2E / (EPS * SCALE))
+    for k in range(1, Q):
+        send_bias(k).start()
+
+    near = (t_hi, t_hi + 1 - 2 * (t_hi % 2), (t_hi + 2) % Q, Q - 1 - t_hi)
+
+    def blocks_of(tile):
+        first = tile * near[1] + (1 - tile) * near[2]
+        second = tile * near[0] + (1 - tile) * near[3]
+        return under(src_t, first * Q + t_lo, second * Q + t_lo)
+
+    high[...] = jnp.full((2, 8, 2 * B), -1e30, F32)
+    mass[...] = jnp.zeros((2, 8, 2 * B), F32)
+    moment[...] = jnp.zeros((2, B, 2 * B), F32)
+
+    def add_moments(tile, j):
+        top, weight, total = moment_step(
+            rows.at[j], rows_t.at[j], bias.at[j], blocks_of(tile), high[tile, pl.ds(0, 1), :], mass[tile], moment[tile]
+        )
+        high[tile] = jnp.broadcast_to(top, (8, 2 * B))
+        mass[tile] = weight
+        moment[tile] = total
+
+    def own_moments(tile, carry):
+        add_moments(tile, 1)
         return carry
 
-    lax.fori_loop(0, Q, last_group, 0)
+    lax.fori_loop(0, 2, own_moments, 0)
+    for k in range(1, Q):
+        send_bias(k).wait_recv()
+        put_bias(bias.at[1 + k], far_bias[k])
+
+    def send_part(r):
+        return copy(part.at[r], got.at[r - 1], r_send.at[r - 1], r_recv.at[r - 1], {"tgt": near[r] * Q + t_lo})
+
+    def far_moments(tile, carry):
+        def step(j, carry):
+            add_moments(tile, j)
+            return carry
+
+        lax.fori_loop(2, 2 + Q - 1, step, 0)
+        weight = jnp.sum(mass[tile], axis=0, keepdims=True)
+        mean = moment[tile] / weight
+        level = high[tile] * SCALE + jnp.log2(weight)
+        for r, cut in ((2 - tile, pl.ds(0, B)), (3 - 3 * tile, pl.ds(B, B))):
+            at = slice(cut.start, cut.start + B)
+            part[r, pl.ds(0, B), :] = mean[:, at]
+            part[r, pl.ds(B, 8), :] = level[:, at]
+
+        @pl.when(tile == 0)
+        def _():
+            send_part(2).start()
+            send_part(3).start()
+
+        return carry
+
+    lax.fori_loop(0, 2, far_moments, 0)
+    send_part(1).start()
 
     def join(pieces):
         levels = [p[pl.ds(B, 8), :] for p in pieces]
-        high = functools.reduce(jnp.maximum, levels)
-        scaled = [jnp.exp2(v - high) for v in levels]
+        top = functools.reduce(jnp.maximum, levels)
+        scaled = [jnp.exp2(v - top) for v in levels]
         total = functools.reduce(jnp.add, scaled)
         out = None
         for p, v in zip(pieces, scaled):
             term = p[pl.ds(0, B), :] * (v / total)[:1, :]
             out = term if out is None else out + term
-        return out, high + jnp.log2(total)
-
-    def send_hi(k):
-        return copy(part2.at[k], got2.at[k - 1], r_send.at[k - 1], r_recv.at[k - 1], hi_peer("tgt", k))
-
-    for k in (1, 2, 3, 0):
-        z = (t_hi + k) % Q
-        for j in range(1, Q):
-            send_lo(j, z).wait_recv()
-        mean, level = join([part.at[0, z]] + [got.at[j, z] for j in range(Q - 1)])
-        part2[k, pl.ds(0, B), :] = mean
-        part2[k, pl.ds(B, 8), :] = level
-        if k > 0:
-            send_hi(k).start()
-    for k in range(1, Q):
-        send_hi(k).wait_recv()
-    mean, level = join([part2.at[0]] + [got2.at[j] for j in range(Q - 1)])
-    map_ref[...] = mean.T
+        return out
+
+    for r in range(1, Q):
+        send_part(r).wait_recv()
+    map_ref[...] = join([part.at[0]] + [got.at[j] for j in range(Q - 1)]).T
 
     for k in range(1, Q):
         gather_hi(k).wait_send()
-        send_hi(k).wait_send()
+        spread(k).wait_send()
+        hand_over(k).wait_send()
+        send_bias(k).wait_send()
+        send_part(k).wait_send()
         for d in range(Q):
             gather_lo(d, k).wait_send()
-            send_lo(k, d).wait_send()
     for e in range(4):
         for h in range(2):
             all_bytes(e, h, e_send).wait()
@@ -321,22 +372,24 @@
         in_specs=[pl.BlockSpec(memory_space=pltpu.HBM)] * 4,
         out_specs=(vmem, vmem, vmem),
         scratch_shapes=[
-            pltpu.VMEM((2, N, D), BF),
-            pltpu.VMEM((2, D, N), BF),
-            pltpu.VMEM((2, N, B), BF),
+            pltpu.VMEM((1 + Q, N, D), BF),
+            pltpu.VMEM((1 + Q, D, N), BF),
+            pltpu.VMEM((1 + Q, N, B), BF),
             pltpu.VMEM((FILL, NB, B), F32),
             pltpu.VMEM((2, NB, B), F32),
             pltpu.VMEM((2, NB, B), F32),
             pltpu.VMEM((4, 2, NB // 2, B), F32),
             pltpu.VMEM((4, 2, NB, NB // 2, B), F32),
-            pltpu.VMEM((Q, Q, B + 8, D), F32),
-            pltpu.VMEM((Q - 1, Q, B + 8, D), F32),
+            pltpu.VMEM((2, B, 2 * B), F32),
+            pltpu.VMEM((2, 8, 2 * B), F32),
+            pltpu.VMEM((2, 8, 2 * B), F32),
+            pltpu.VMEM((Q, NB, B), F32),
             pltpu.VMEM((Q, B + 8, D), F32),
             pltpu.VMEM((Q - 1, B + 8, D), F32),
             dma((4,)),
             dma((Q - 1,)), dma((Q - 1,)), dma((Q, Q - 1)), dma((Q, Q - 1)),
             dma((4, 2)), dma((4, 2)),
-            dma((Q - 1, Q)), dma((Q - 1, Q)), dma((Q - 1,)), dma((Q - 1,)),
+            *[dma((Q - 1,))] * 8,
         ],
         compiler_params=pltpu.CompilerParams(
             collective_id=0, has_side_effects=True, vmem_limit_bytes=64 * 1024 * 1024

time: 87.9 us -> 81.7 us (0.929)
  Pallas kernels: 83.5 us -> 78.1 us
    pallas_call x1, Pallas kernels: 83.5 us -> 78.1 us  [shards(): pl.pallas_call(kernel, out_shape=(jax.ShapeDtypeStruct((B, D), F32), jax....]
where the time goes in v4:
time: 81.7 us; the launch traced here: 81.5 us
  Pallas kernels  78.1 us (96%)
  local copies, waits for them, and re-layouts  2.78 us (3%)
    pallas_call x1, Pallas kernels, shards(): pl.pallas_call(kernel, out_shape=(jax.ShapeDtypeStruct((B, D), F32), jax....  78.1 us
    unnamed x7, local copies, waits for them, and re-layouts  2.78 us

profile of v4, /device:TPU:1, one launch (start us, length us, event | category | flops | bytes accessed | tf_op | source)
XLA Modules:
  0.0 81.5 jit_solution(16300622237429937308)
XLA Ops:
  0.6 78.1 %shard_map.67 = (f32[128,128]{1,0:T(8,128)}, f32[16,128]{1,0:T(8,128)}, f32[16,128]{1,0:T(8,128)}) custom-call(bf16[128,128]{1,0:T(8,128)(2,1)} %src_hbm.1, bf16[2048,128]{1,0:T(8,128)(2,1)} %tgt_hbm.1, f32[16,128]{1,0:T(8,128)} %bitcast.4, f32[16,128]{1,0:T(8,128)} %bitcast.5), custom_call_target="tpu_custom_call" | custom-call | tf_op jit(solution)/shard_map/pallas_call | solution.py:365
  78.8 0.0 copy-start.1
  78.8 1.5 %copy.10 = f32[128,128]{1,0:T(8,128)} copy(f32[128,128]{1,0:T(8,128)} %get-tuple-element.12) | data formatting | bytes 131072
  80.2 0.0 copy-done.1
  80.2 0.0 copy-start
  80.2 0.6 copy.11
  80.8 0.1 copy-done
  80.9 0.6 copy.12
Async XLA Ops:
  78.8 1.5 %copy-start.1 = (f32[16,128]{1,0:T(8,128)S(1)}, f32[16,128]{1,0:T(8,128)}, u32[]{:S(2)}) copy-start(f32[16,128]{1,0:T(8,128)} %get-tuple-element.7) | copy-start | bytes 24580
  80.2 0.7 copy-start

commit v5 on v4

--- a/solution.py
+++ b/solution.py
@@ -21,7 +21,7 @@
 F32 = jnp.float32
 
 
-FILL = 6880
+FILL = 6860
 GROUP = 16
 
 
@@ -31,23 +31,30 @@
     return jnp.maximum(x[:half], x[half:]) if op is jnp.max else x[:half] + x[half:]
 
 
-def lse_tile(rows, bias, rhs):
-    high = None
-    for q in range(NB):
-        at = pl.ds(q * B, B)
+def lse_chunks(rows, bias, rhs, first, count, high, total):
+    for q in range(count):
+        at = pl.ds(pl.multiple_of((first + q) * B, B), B)
         u = jnp.dot(jnp.concatenate([rows[at, :], bias[at, :]], axis=1), rhs, preferred_element_type=F32)
-        new = fold(u, jnp.max)
-        if high is not None:
-            new = jnp.maximum(high, new)
+        new = jnp.maximum(high, fold(u, jnp.max))
         part = jnp.exp2((u.reshape(B // 8, 8, u.shape[1]) - new[None]) * SCALE).reshape(u.shape)
-        part = fold(part, jnp.sum)
-        total = part if high is None else total * jnp.exp2((high - new) * SCALE) + part
+        total = total * jnp.exp2((high - new) * SCALE) + fold(part, jnp.sum)
         high = new
+    return high, total
+
+
+def lse_end(high, total):
     y = high * SCALE + jnp.log2(total)
     top = jnp.max(y, axis=0, keepdims=True)
     return top + jnp.log2(jnp.sum(jnp.exp2(y - top), axis=0, keepdims=True))
 
 
+def lse_tile(rows, bias, rhs):
+    start = jnp.full((8, rhs.shape[1]), LOW, F32), jnp.zeros((8, rhs.shape[1]), F32)
+    return lse_end(*lse_chunks(rows, bias, rhs, 0, NB, *start))
+
+
+LOW = -1e30
+HALF = NB // 2
 CHUNK = 256
 UNROLL = 4
 
@@ -72,7 +79,7 @@
 def kernel(
     src_hbm, tgt_hbm, slm_hbm, tlm_hbm, map_ref, sd_ref, td_ref,
     rows, rows_t, bias, logmass, norm, dual, vec, inbox,
-    moment, mass, high, far_bias, part, got, in_sem,
+    run_high, run_total, moment, mass, high, far_bias, part, got, in_sem,
     g_hi_send, g_hi_recv, g_lo_send, g_lo_recv,
     e_send, e_recv, x_send, x_recv, f_send, f_recv, b_send, b_recv, r_send, r_recv,
 ):
@@ -126,14 +133,14 @@
     lane = lax.broadcasted_iota(jnp.int32, (B, B), 1)
     ones = jnp.ones((D, 2 * B), BF)
 
-    def put_bias(out, bias):
-        hi = bias.astype(BF).astype(F32)
-        rest = bias - hi
+    def put_bias(out, values, half):
+        hi = values.astype(BF).astype(F32)
+        rest = values - hi
         mid = rest.astype(BF).astype(F32)
         low = rest - mid
-        turned = jnp.concatenate([hi, mid, low, jnp.zeros((B - 3 * NB, B), F32)], axis=0).T
-        for k in range(NB):
-            out[pl.ds(k * B, B), :] = jnp.where(lane % NB == k, turned, 0.0).astype(BF)
+        turned = jnp.concatenate([hi, mid, low, jnp.zeros((B - 3 * HALF, B), F32)], axis=0).T
+        for k in range(HALF):
+            out[block_at(half * HALF + k), :] = jnp.where(lane % HALF == k, turned, 0.0).astype(BF)
 
     def turn(rows, rows_t, norm, at):
         turned = rows.astype(F32).T
@@ -155,7 +162,8 @@
         f.wait()
     for k in range(NB):
         turn(tgt_ref[pl.ds(k * B, B), :], tgt_t, tgt_norm, k)
-    put_bias(tgt_bias, tgt_norm[...] * (-LOG2E / (EPS * SCALE)))
+    for half in range(2):
+        put_bias(tgt_bias, tgt_norm[pl.ds(half * HALF, HALF), :] * (-LOG2E / (EPS * SCALE)), half)
 
     def take(at):
         turn(codes[block_at(at), :], src_t, src_norm, at)
@@ -201,16 +209,16 @@
         others = inbox.at[e, h, pl.ds(0, NB - 1)]
         return pltpu.make_async_copy(others, others, sem.at[e, h])
 
-    def receive(e):
-        for h in range(2):
-            all_bytes(e, h, e_recv).wait()
-        pieces = [inbox[e, :, k].reshape(NB, B) for k in range(NB)]
-        high = functools.reduce(jnp.maximum, pieces)
-        level = high + jnp.log2(functools.reduce(jnp.add, [jnp.exp2(p - high) for p in pieces]))
+    def receive(e, h):
+        all_bytes(e, h, e_recv).wait()
+        pieces = [inbox[e, h, k] for k in range(NB)]
+        top = functools.reduce(jnp.maximum, pieces)
+        level = top + jnp.log2(functools.reduce(jnp.add, [jnp.exp2(p - top) for p in pieces]))
         side = e % 2
-        log = logmass[side] * LOG2E - level
-        put_bias(bias.at[side], log * (1.0 / SCALE))
-        dual[side] = log * (EPS / LOG2E) + norm[side]
+        here = pl.ds(pl.multiple_of(h * HALF, HALF), HALF)
+        log = logmass[side, here, :] * LOG2E - level
+        put_bias(bias.at[side], log * (1.0 / SCALE), h)
+        dual[side, here, :] = log * (EPS / LOG2E) + norm[side, here, :]
 
     half_rows = pl.ds(pl.multiple_of(src_me % 2 * (N // 2), N // 2), N // 2)
 
@@ -222,28 +230,51 @@
         return copy(there, there, f_send.at[k - 1], f_recv.at[k - 1], {"src": src_me + 1 - 2 * (src_me % 2)})
 
     def whole_pass(e, carry):
-        receive(e - 1)
-
-        @pl.when(e == 1)
-        def _():
-            for k in range(1, Q):
-                spread(k).start()
-
         side = (e - 1) % 2
-
-        def half(h, carry):
+        late = jnp.minimum(e - 1, 1)
+        run_high[...] = jnp.full((8, N), LOW, F32)
+        run_total[...] = jnp.zeros((8, N), F32)
+
+        def quarter(s, carry):
+            slow, fast = s // 2, s % 2
+            h = late * fast + (1 - late) * slow
+            m = late * slow + (1 - late) * fast
+
+            @pl.when(s == 0)
+            def _():
+                receive(e - 1, 0)
+
+            @pl.when(s == 2 * late)
+            def _():
+                receive(e - 1, 1)
+
+            @pl.when((s == 0) & (e == 1))
+            def _():
+                for k in range(1, Q):
+                    spread(k).start()
+
             def body(k, carry):
-                at = h * (NB // 4) + k
-                total = lse_tile(rows.at[side], bias.at[side], under(rows_t.at[1 - side], 2 * at, 2 * at + 1))
-                vec[e, h, pl.ds(2 * k, 1), :] = total[:, :B]
-                vec[e, h, pl.ds(2 * k + 1, 1), :] = total[:, B:]
+                at = h * (HALF // 2) + k
+                here = pl.ds(pl.multiple_of(at * 2 * B, 2 * B), 2 * B)
+                rhs = under(rows_t.at[1 - side], 2 * at, 2 * at + 1)
+                run_high[:, here], run_total[:, here] = lse_chunks(
+                    rows.at[side], bias.at[side], rhs, m * HALF, HALF, run_high[:, here], run_total[:, here]
+                )
                 return carry
 
-            lax.fori_loop(0, NB // 4, body, 0, unroll=UNROLL)
-            send_half(e, h)
+            lax.fori_loop(0, HALF // 2, body, 0, unroll=UNROLL)
+
+            @pl.when(m == 1)
+            def _():
+                here = pl.ds(pl.multiple_of(h * (N // 2), N // 2), N // 2)
+                out = lse_end(run_high[:, here], run_total[:, here])
+                for k in range(HALF):
+                    vec[e, h, pl.ds(k, 1), :] = out[:, k * B : (k + 1) * B]
+                send_half(e, h)
+
             return carry
 
-        lax.fori_loop(0, 2, half, 0)
+        lax.fori_loop(0, 4, quarter, 0)
 
         @pl.when(e == 2)
         def _():
@@ -265,7 +296,8 @@
         return carry
 
     lax.fori_loop(2, 2 + Q - 1, turn_far, 0)
-    receive(3)
+    receive(3, 0)
+    receive(3, 1)
     sd_ref[...] = dual[0]
     td_ref[...] = dual[1]
 
@@ -283,7 +315,7 @@
         second = tile * near[0] + (1 - tile) * near[3]
         return under(src_t, first * Q + t_lo, second * Q + t_lo)
 
-    high[...] = jnp.full((2, 8, 2 * B), -1e30, F32)
+    high[...] = jnp.full((2, 8, 2 * B), LOW, F32)
     mass[...] = jnp.zeros((2, 8, 2 * B), F32)
     moment[...] = jnp.zeros((2, B, 2 * B), F32)
 
@@ -302,7 +334,8 @@
     lax.fori_loop(0, 2, own_moments, 0)
     for k in range(1, Q):
         send_bias(k).wait_recv()
-        put_bias(bias.at[1 + k], far_bias[k])
+        for half in range(2):
+            put_bias(bias.at[1 + k], far_bias[k, pl.ds(half * HALF, HALF), :], half)
 
     def send_part(r):
         return copy(part.at[r], got.at[r - 1], r_send.at[r - 1], r_recv.at[r - 1], {"tgt": near[r] * Q + t_lo})
@@ -359,16 +392,23 @@
             all_bytes(e, h, e_send).wait()
 
 
+def hand_on(mapped, src_dual, tgt_dual, mapped_out, src_out, tgt_out):
+    mapped_out[...] = mapped[...]
+    src_out[...] = src_dual[...]
+    tgt_out[...] = tgt_dual[...]
+
+
 def shards(sources, targets, src_logmass, tgt_logmass):
     vmem = pl.BlockSpec(memory_space=pltpu.VMEM)
     dma = pltpu.SemaphoreType.DMA
-    mapped, src_dual, tgt_dual = pl.pallas_call(
+    results = (
+        jax.ShapeDtypeStruct((B, D), F32),
+        jax.ShapeDtypeStruct((NB, B), F32),
+        jax.ShapeDtypeStruct((NB, B), F32),
+    )
+    found = pl.pallas_call(
         kernel,
-        out_shape=(
-            jax.ShapeDtypeStruct((B, D), F32),
-            jax.ShapeDtypeStruct((NB, B), F32),
-            jax.ShapeDtypeStruct((NB, B), F32),
-        ),
+        out_shape=results,
         in_specs=[pl.BlockSpec(memory_space=pltpu.HBM)] * 4,
         out_specs=(vmem, vmem, vmem),
         scratch_shapes=[
@@ -380,6 +420,8 @@
             pltpu.VMEM((2, NB, B), F32),
             pltpu.VMEM((4, 2, NB // 2, B), F32),
             pltpu.VMEM((4, 2, NB, NB // 2, B), F32),
+            pltpu.VMEM((8, N), F32),
+            pltpu.VMEM((8, N), F32),
             pltpu.VMEM((2, B, 2 * B), F32),
             pltpu.VMEM((2, 8, 2 * B), F32),
             pltpu.VMEM((2, 8, 2 * B), F32),
@@ -395,6 +437,12 @@
             collective_id=0, has_side_effects=True, vmem_limit_bytes=64 * 1024 * 1024
         ),
     )(sources, targets, src_logmass.reshape(NB, B), tgt_logmass.reshape(NB, B))
+    mapped, src_dual, tgt_dual = pl.pallas_call(
+        hand_on,
+        out_shape=results,
+        in_specs=[vmem] * 3,
+        out_specs=(vmem,) * 3,
+    )(*found)
     return mapped, src_dual.reshape(N), tgt_dual.reshape(N)
 
 

time: 81.7 us -> 77 us (0.942)
  local copies, waits for them, and re-layouts: 2.78 us -> 0 us
  Pallas kernels: 78.1 us -> 76.3 us
    unnamed x7 -> x0, local copies, waits for them, and re-layouts: 2.78 us -> none
    pallas_call x1 -> x2, Pallas kernels: 78.1 us -> 76.3 us  [the longest x1 74.8 us: shards(): pl.pallas_call(kernel, out_shape=results, in_specs=[pl.BlockSpec(memory_s...]
where the time goes in v5:
time: 77 us; the launch traced here: 76.9 us
  Pallas kernels  76.3 us (99%)
    pallas_call x1, Pallas kernels, shards(): pl.pallas_call(kernel, out_shape=results, in_specs=[pl.BlockSpec(memory_s...  74.8 us

profile of v5, /device:TPU:1, one launch (start us, length us, event | category | flops | bytes accessed | tf_op | source)
XLA Modules:
  0.0 76.9 jit_solution(15831896149255641061)
XLA Ops:
  0.6 74.8 %shard_map.67 = (f32[128,128]{1,0:T(8,128)}, f32[16,128]{1,0:T(8,128)}, f32[16,128]{1,0:T(8,128)}) custom-call(bf16[128,128]{1,0:T(8,128)(2,1)} %src_hbm.1, bf16[2048,128]{1,0:T(8,128)(2,1)} %tgt_hbm.1, f32[16,128]{1,0:T(8,128)} %bitcast.4, f32[16,128]{1,0:T(8,128)} %bitcast.5), custom_call_target="tpu_custom_call" | custom-call | tf_op jit(solution)/shard_map/pallas_call | solution.py:409
  75.4 1.5 %shard_map.68 = (f32[128,128]{1,0:T(8,128)}, f32[16,128]{1,0:T(8,128)}, f32[16,128]{1,0:T(8,128)}) custom-call(f32[128,128]{1,0:T(8,128)} %get-tuple-element.9.mapped, f32[16,128]{1,0:T(8,128)} %get-tuple-element.10.src_dual, f32[16,128]{1,0:T(8,128)} %get-tuple-element.11.tgt_dual), custom_call_target="tpu_custom_call" | custom-call | tf_op jit(solution)/shard_map/pallas_call | solution.py:440

commit v6 on v5

--- a/solution.py
+++ b/solution.py
@@ -112,9 +112,22 @@
         f.start()
 
     barrier = pltpu.get_barrier_semaphore()
-    for k in range(1, NB):
-        for axis, me in (("tgt", tgt_me), ("src", src_me)):
-            pl.semaphore_signal(barrier, 1, device_id={axis: (me + k) % NB}, device_id_type=MESH)
+    for k in range(1, Q):
+        pl.semaphore_signal(barrier, 1, device_id=lo_peer("tgt", k), device_id_type=MESH)
+        pl.semaphore_signal(barrier, 1, device_id=hi_peer("tgt", k), device_id_type=MESH)
+    side, core = s_lo // 2, s_lo % 2
+    edge = (Q - 1) * (1 - t_hi // 2)
+    for k in range(Q):
+        for c in range(2):
+            row, other = ((s_hi + k) % Q) * Q, (core + c) % 2
+            if k or c:
+                pl.semaphore_signal(
+                    barrier, 1, device_id=(row + side * 2 + other, tgt_me), device_id_type=MESH
+                )
+            pl.semaphore_signal(
+                barrier, 1, device_id=(row + (1 - side) * 2 + other, edge * Q + t_lo), device_id_type=MESH
+            )
+    greeted = 2 * (Q - 1) + 2 * Q - 1 + 4 * Q * (1 - (t_hi + 1) // 2 % 2)
 
     def copy(src, dst, send, recv, peer):
         return pltpu.make_async_remote_copy(
@@ -152,7 +165,7 @@
         return jnp.concatenate([pair, ones], axis=0)
 
     fetches[0].wait()
-    pl.semaphore_wait(barrier, 2 * (NB - 1))
+    pl.semaphore_wait(barrier, greeted)
     for k in range(1, Q):
         gather_hi(k).start()
     for k in range(1, Q):

time: 77 us -> 76.3 us (level)
  Pallas kernels: 76.3 us -> 75.5 us
where the time goes in v6:
time: 76.3 us; the launch traced here: 76.1 us
  Pallas kernels  75.5 us (99%)
    pallas_call x1, Pallas kernels, shards(): pl.pallas_call(kernel, out_shape=results, in_specs=[pl.BlockSpec(memory_s...  74 us

profile of v6, /device:TPU:1, one launch (start us, length us, event | category | flops | bytes accessed | tf_op | source)
XLA Modules:
  0.0 76.1 jit_solution(12465925009799283047)
XLA Ops:
  0.6 74.0 %shard_map.67 = (f32[128,128]{1,0:T(8,128)}, f32[16,128]{1,0:T(8,128)}, f32[16,128]{1,0:T(8,128)}) custom-call(bf16[128,128]{1,0:T(8,128)(2,1)} %src_hbm.1, bf16[2048,128]{1,0:T(8,128)(2,1)} %tgt_hbm.1, f32[16,128]{1,0:T(8,128)} %bitcast.4, f32[16,128]{1,0:T(8,128)} %bitcast.5), custom_call_target="tpu_custom_call" | custom-call | tf_op jit(solution)/shard_map/pallas_call | solution.py:422
  74.7 1.5 %shard_map.68 = (f32[128,128]{1,0:T(8,128)}, f32[16,128]{1,0:T(8,128)}, f32[16,128]{1,0:T(8,128)}) custom-call(f32[128,128]{1,0:T(8,128)} %get-tuple-element.9.mapped, f32[16,128]{1,0:T(8,128)} %get-tuple-element.10.src_dual, f32[16,128]{1,0:T(8,128)} %get-tuple-element.11.tgt_dual), custom_call_target="tpu_custom_call" | custom-call | tf_op jit(solution)/shard_map/pallas_call | solution.py:453

commit v7 on v5

--- a/solution.py
+++ b/solution.py
@@ -79,7 +79,7 @@
 def kernel(
     src_hbm, tgt_hbm, slm_hbm, tlm_hbm, map_ref, sd_ref, td_ref,
     rows, rows_t, bias, logmass, norm, dual, vec, inbox,
-    run_high, run_total, moment, mass, high, far_bias, part, got, in_sem,
+    run_high, run_total, moment, mass, high, far_bias, part, got, in_sem, here_sem,
     g_hi_send, g_hi_recv, g_lo_send, g_lo_recv,
     e_send, e_recv, x_send, x_recv, f_send, f_recv, b_send, b_recv, r_send, r_recv,
 ):
@@ -112,9 +112,25 @@
         f.start()
 
     barrier = pltpu.get_barrier_semaphore()
-    for k in range(1, NB):
-        for axis, me in (("tgt", tgt_me), ("src", src_me)):
-            pl.semaphore_signal(barrier, 1, device_id={axis: (me + k) % NB}, device_id_type=MESH)
+    side, core = s_lo // 2, s_lo % 2
+    is_edge = t_hi == (Q - 1) * (1 - side)
+    near_src = [
+        {"src": ((s_hi + k) % Q) * Q + side * 2 + (core + c) % 2} for k in range(Q) for c in range(2) if k or c
+    ]
+    across = (s_hi * Q + (1 - side) * 2 + core, (Q - 1 - t_hi) * Q + t_lo)
+    hi_peers = [hi_peer("tgt", k) for k in range(1, Q)]
+
+    def signal_all(sem, peers):
+        for peer in peers:
+            pl.semaphore_signal(sem, 1, device_id=peer, device_id_type=MESH)
+
+    signal_all(barrier, hi_peers + [lo_peer("tgt", k) for k in range(1, Q)] + near_src)
+
+    @pl.when(is_edge)
+    def _():
+        signal_all(barrier, [across])
+
+    greeted = 2 * (Q - 1) + len(near_src) + 1 - jnp.minimum(jnp.abs(t_hi - (Q - 1) * (1 - side)), 1)
 
     def copy(src, dst, send, recv, peer):
         return pltpu.make_async_remote_copy(
@@ -152,7 +168,7 @@
         return jnp.concatenate([pair, ones], axis=0)
 
     fetches[0].wait()
-    pl.semaphore_wait(barrier, 2 * (NB - 1))
+    pl.semaphore_wait(barrier, greeted)
     for k in range(1, Q):
         gather_hi(k).start()
     for k in range(1, Q):
@@ -177,6 +193,10 @@
         gather_hi(d).wait_recv()
         for k in range(1, Q):
             gather_lo(d, k).start()
+
+    @pl.when(is_edge)
+    def _():
+        signal_all(here_sem.at[0], [across])
 
     def first_group(d, carry):
         hi = (t_hi - d + Q) % Q
@@ -190,6 +210,12 @@
         gather_lo(d, 3).wait_recv()
         take(at[3])
         first_pair(at[2], at[3])
+
+        @pl.when(is_edge & (d == 2))
+        def _():
+            pl.semaphore_wait(here_sem.at[0], 1)
+            signal_all(here_sem.at[1], near_src)
+
         return carry
 
     lax.fori_loop(0, Q, first_group, 0)
@@ -248,6 +274,10 @@
             def _():
                 receive(e - 1, 1)
 
+            @pl.when((s == 0) & (e == 1) & ~is_edge)
+            def _():
+                pl.semaphore_wait(here_sem.at[2], 1)
+
             @pl.when((s == 0) & (e == 1))
             def _():
                 for k in range(1, Q):
@@ -286,6 +316,12 @@
 
     send_half(0, 0)
     send_half(0, 1)
+
+    @pl.when(is_edge)
+    def _():
+        pl.semaphore_wait(here_sem.at[1], len(near_src))
+        signal_all(here_sem.at[2], hi_peers)
+
     lax.fori_loop(1, 4, whole_pass, 0)
     for k in range(1, Q):
         hand_over(k).wait_recv()
@@ -428,7 +464,7 @@
             pltpu.VMEM((Q, NB, B), F32),
             pltpu.VMEM((Q, B + 8, D), F32),
             pltpu.VMEM((Q - 1, B + 8, D), F32),
-            dma((4,)),
+            dma((4,)), pltpu.SemaphoreType.REGULAR((3,)),
             dma((Q - 1,)), dma((Q - 1,)), dma((Q, Q - 1)), dma((Q, Q - 1)),
             dma((4, 2)), dma((4, 2)),
             *[dma((Q - 1,))] * 8,

time: 77 us -> 72.9 us (0.947)
  Pallas kernels: 76.3 us -> 72.1 us
    pallas_call x1, Pallas kernels: 74.8 us -> 70.6 us  [shards(): pl.pallas_call(kernel, out_shape=results, in_specs=[pl.BlockSpec(memory_s...]
where the time goes in v7:
time: 72.9 us; the launch traced here: 72.8 us
  Pallas kernels  72.1 us (99%)
    pallas_call x1, Pallas kernels, shards(): pl.pallas_call(kernel, out_shape=results, in_specs=[pl.BlockSpec(memory_s...  70.6 us
    pallas_call x1, Pallas kernels, shards(): pl.pallas_call(hand_on, out_shape=results, in_specs=[vmem] * 3, out_specs...  1.5 us

profile of v7, /device:TPU:1, one launch (start us, length us, event | category | flops | bytes accessed | tf_op | source)
XLA Modules:
  0.0 72.8 jit_solution(17285547403079193154)
XLA Ops:
  0.6 70.6 %shard_map.67 = (f32[128,128]{1,0:T(8,128)}, f32[16,128]{1,0:T(8,128)}, f32[16,128]{1,0:T(8,128)}) custom-call(bf16[128,128]{1,0:T(8,128)(2,1)} %src_hbm.1, bf16[2048,128]{1,0:T(8,128)(2,1)} %tgt_hbm.1, f32[16,128]{1,0:T(8,128)} %bitcast.4, f32[16,128]{1,0:T(8,128)} %bitcast.5), custom_call_target="tpu_custom_call" | custom-call | tf_op jit(solution)/shard_map/pallas_call | solution.py:445
  71.3 1.5 %shard_map.68 = (f32[128,128]{1,0:T(8,128)}, f32[16,128]{1,0:T(8,128)}, f32[16,128]{1,0:T(8,128)}) custom-call(f32[128,128]{1,0:T(8,128)} %get-tuple-element.9.mapped, f32[16,128]{1,0:T(8,128)} %get-tuple-element.10.src_dual, f32[16,128]{1,0:T(8,128)} %get-tuple-element.11.tgt_dual), custom_call_target="tpu_custom_call" | custom-call | tf_op jit(solution)/shard_map/pallas_call | solution.py:476

commit v8 on v7

--- a/solution.py
+++ b/solution.py
@@ -21,7 +21,7 @@
 F32 = jnp.float32
 
 
-FILL = 6860
+FILL = 6760
 GROUP = 16
 
 
@@ -368,20 +368,30 @@
         return carry
 
     lax.fori_loop(0, 2, own_moments, 0)
-    for k in range(1, Q):
+
+    def take_bias(k):
         send_bias(k).wait_recv()
         for half in range(2):
             put_bias(bias.at[1 + k], far_bias[k, pl.ds(half * HALF, HALF), :], half)
 
+    take_bias(1)
+    take_bias(3)
+
     def send_part(r):
         return copy(part.at[r], got.at[r - 1], r_send.at[r - 1], r_recv.at[r - 1], {"tgt": near[r] * Q + t_lo})
 
     def far_moments(tile, carry):
         def step(j, carry):
-            add_moments(tile, j)
+            add_moments(tile, 2 + 2 * j)
             return carry
 
-        lax.fori_loop(2, 2 + Q - 1, step, 0)
+        lax.fori_loop(0, 2, step, 0)
+
+        @pl.when(tile == 0)
+        def _():
+            take_bias(2)
+
+        add_moments(tile, 3)
         weight = jnp.sum(mass[tile], axis=0, keepdims=True)
         mean = moment[tile] / weight
         level = high[tile] * SCALE + jnp.log2(weight)

time: 72.9 us -> 72.9 us (level)
  no operation moved by 1% of the time
where the time goes in v8:
time: 72.9 us; the launch traced here: 72.8 us
  Pallas kernels  72.1 us (99%)
    pallas_call x1, Pallas kernels, shards(): pl.pallas_call(kernel, out_shape=results, in_specs=[pl.BlockSpec(memory_s...  70.6 us
    pallas_call x1, Pallas kernels, shards(): pl.pallas_call(hand_on, out_shape=results, in_specs=[vmem] * 3, out_specs...  1.5 us

profile of v8, /device:TPU:1, one launch (start us, length us, event | category | flops | bytes accessed | tf_op | source)
XLA Modules:
  0.0 72.8 jit_solution(1381924824679521013)
XLA Ops:
  0.6 70.6 %shard_map.67 = (f32[128,128]{1,0:T(8,128)}, f32[16,128]{1,0:T(8,128)}, f32[16,128]{1,0:T(8,128)}) custom-call(bf16[128,128]{1,0:T(8,128)(2,1)} %src_hbm.1, bf16[2048,128]{1,0:T(8,128)(2,1)} %tgt_hbm.1, f32[16,128]{1,0:T(8,128)} %bitcast.4, f32[16,128]{1,0:T(8,128)} %bitcast.5), custom_call_target="tpu_custom_call" | custom-call | tf_op jit(solution)/shard_map/pallas_call | solution.py:455
  71.3 1.5 %shard_map.68 = (f32[128,128]{1,0:T(8,128)}, f32[16,128]{1,0:T(8,128)}, f32[16,128]{1,0:T(8,128)}) custom-call(f32[128,128]{1,0:T(8,128)} %get-tuple-element.9.mapped, f32[16,128]{1,0:T(8,128)} %get-tuple-element.10.src_dual, f32[16,128]{1,0:T(8,128)} %get-tuple-element.11.tgt_dual), custom_call_target="tpu_custom_call" | custom-call | tf_op jit(solution)/shard_map/pallas_call | solution.py:486

commit v9 on v8

--- a/solution.py
+++ b/solution.py
@@ -205,11 +205,11 @@
         gather_lo(d, 1).wait_recv()
         take(at[1])
         first_pair(at[0], at[1])
+        gather_lo(d, 3).wait_recv()
+        take(at[3])
         gather_lo(d, 2).wait_recv()
         take(at[2])
-        gather_lo(d, 3).wait_recv()
-        take(at[3])
-        first_pair(at[2], at[3])
+        first_pair(at[3], at[2])
 
         @pl.when(is_edge & (d == 2))
         def _():

time: 72.9 us -> 72.9 us (level)
  no operation moved by 1% of the time
where the time goes in v9:
time: 72.9 us; the launch traced here: 72.8 us
  Pallas kernels  72.2 us (99%)
    pallas_call x1, Pallas kernels, shards(): pl.pallas_call(kernel, out_shape=results, in_specs=[pl.BlockSpec(memory_s...  70.7 us
    pallas_call x1, Pallas kernels, shards(): pl.pallas_call(hand_on, out_shape=results, in_specs=[vmem] * 3, out_specs...  1.5 us

profile of v9, /device:TPU:1, one launch (start us, length us, event | category | flops | bytes accessed | tf_op | source)
XLA Modules:
  0.0 72.8 jit_solution(15754163261108033272)
XLA Ops:
  0.6 70.7 %shard_map.67 = (f32[128,128]{1,0:T(8,128)}, f32[16,128]{1,0:T(8,128)}, f32[16,128]{1,0:T(8,128)}) custom-call(bf16[128,128]{1,0:T(8,128)(2,1)} %src_hbm.1, bf16[2048,128]{1,0:T(8,128)(2,1)} %tgt_hbm.1, f32[16,128]{1,0:T(8,128)} %bitcast.4, f32[16,128]{1,0:T(8,128)} %bitcast.5), custom_call_target="tpu_custom_call" | custom-call | tf_op jit(solution)/shard_map/pallas_call | solution.py:455
  71.3 1.5 %shard_map.68 = (f32[128,128]{1,0:T(8,128)}, f32[16,128]{1,0:T(8,128)}, f32[16,128]{1,0:T(8,128)}) custom-call(f32[128,128]{1,0:T(8,128)} %get-tuple-element.9.mapped, f32[16,128]{1,0:T(8,128)} %get-tuple-element.10.src_dual, f32[16,128]{1,0:T(8,128)} %get-tuple-element.11.tgt_dual), custom_call_target="tpu_custom_call" | custom-call | tf_op jit(solution)/shard_map/pallas_call | solution.py:486
